TPU v7x, 512 devices: a whole 4x4x16 slice. The times are simulated.
512 devices in a mesh: row: 32 (over z, x_lo), col: 16 (over x_hi, y, core).
Axes of the slice: x: 4 (x_hi: 2, x_lo: 2; x = x_hi * 2 + x_lo), y: 4, z: 16, core: 2. Of those that a mesh axis runs over, the one named last changes fastest.
Arguments:
- image: bfloat16 [256, 256, 256], P('row', 'col'), may hold values from -6 to 6
- w_qkv: bfloat16 [256, 768], replicated, may hold values from -0.375 to 0.375
- w_out: bfloat16 [256, 256], replicated, may hold values from -0.375 to 0.375
- norm_gain: float32 [256], replicated, may hold values from 0.25 to 1.75
- head_scale: float32 [4], replicated, may hold values from 4 to 12
- cotangent: bfloat16 [256, 256, 256], P('row', 'col'), may hold values from -6 to 6
Outputs:
- output: bfloat16 [256, 256, 256], P('row', 'col')
- grad_image: bfloat16 [256, 256, 256], P('row', 'col')
- grad_qkv: float32 [256, 768], replicated
- grad_out: float32 [256, 256], replicated
- grad_gain: float32 [256], replicated
- grad_scale: float32 [4], replicated
All inputs are finite; a program needn't handle non-finite values.
Results may differ from a plain program's by a relative error of at most 0.0093.
Values may be sent and summed in bfloat16 or wider, within the bound.
A program may use at most 64 MiB of HBM per device.

v0:
```python
import math

import jax
import jax.numpy as jnp
from jax import lax
from jax.sharding import PartitionSpec as P

C = 256
HEADS = 4
HEAD_DIM = 64
RADIUS = 3
TH = 8
TW = 16


EPS_NORM = 1e-06
EPS_UNIT = 1e-06


def padded(cells, sides, width):
    for axis, dim in sides:
        count = lax.axis_size(axis)
        ends = count - 1
        head = lax.slice_in_dim(cells, 0, width, axis=dim)
        tail = lax.slice_in_dim(cells, cells.shape[dim] - width, cells.shape[dim], axis=dim)
        cells = jnp.concatenate(
            [
                lax.ppermute(tail, axis, [(i, (i + 1) % count) for i in range(ends)]),
                cells,
                lax.ppermute(head, axis, [((i + 1) % count, i) for i in range(ends)]),
            ],
            axis=dim,
        )
    return cells


def rms_norm(values, norm_gain):
    inverse = lax.rsqrt(jnp.mean(values * values, axis=-1, keepdims=True) + EPS_NORM)
    return values * inverse * norm_gain


def unit_parts(values):
    per_head = values.reshape(values.shape[:-1] + (HEADS, HEAD_DIM))
    inverse = lax.rsqrt(jnp.sum(per_head * per_head, axis=-1, keepdims=True) + EPS_UNIT)
    return (per_head * inverse, inverse)


def unit_backward(unit_value, inverse, grad_unit):
    along = jnp.sum(unit_value * grad_unit, axis=-1, keepdims=True)
    return (grad_unit - unit_value * along) * inverse


def to_lanes(values, length):
    return (
        values.reshape(length, values.shape[-1])
        .T.astype(jnp.float32)
        .reshape(HEADS, HEAD_DIM, length)
    )


def lane_units(values):
    inverse = lax.rsqrt(jnp.sum(values * values, axis=1, keepdims=True) + EPS_UNIT)
    return (values * inverse, inverse)


def band_mask(count, start, stop):
    places = jnp.arange(count, dtype=jnp.int32)
    return (places >= start) & (places < stop)


def on_device(image, w_qkv, w_out, norm_gain, head_scale, cotangent):
    span = 2 * RADIUS + 1
    height = TH * lax.axis_size("row")
    breadth = TW * lax.axis_size("col")
    image_float = image.astype(jnp.float32)
    normed = rms_norm(image_float, norm_gain).astype(jnp.bfloat16)
    packed = jnp.dot(normed, w_qkv, preferred_element_type=jnp.float32).astype(jnp.bfloat16)
    margin = RADIUS
    query_source = packed[:, :, :C]
    key_source = padded(packed[:, :, C:], (("row", 0), ("col", 1)), RADIUS)
    key_rows = TH + 2 * margin
    key_cols = TW + 2 * margin
    length = key_rows * key_cols
    reach = RADIUS * key_cols + RADIUS
    border = ((RADIUS, RADIUS), (RADIUS, RADIUS), (0, 0))
    row_ids = lax.axis_index("row") * TH - margin + jnp.arange(key_rows, dtype=jnp.int32)
    col_ids = lax.axis_index("col") * TW - margin + jnp.arange(key_cols, dtype=jnp.int32)
    row_ok = (row_ids >= 0) & (row_ids < height)
    col_ok = (col_ids >= 0) & (col_ids < breadth)
    inside = (row_ok[:, None] & col_ok[None, :]).astype(jnp.float32).reshape(length)
    query_ok = (
        (
            band_mask(key_rows, RADIUS, key_rows - RADIUS)[:, None]
            & band_mask(key_cols, RADIUS, key_cols - RADIUS)[None, :]
        )
        .astype(jnp.float32)
        .reshape(length)
    )
    own_ok = (
        (
            band_mask(key_rows, margin, margin + TH)[:, None]
            & band_mask(key_cols, margin, margin + TW)[None, :]
        )
        .astype(jnp.float32)
        .reshape(length)
    )
    query_lanes = to_lanes(jnp.pad(query_source, border), length)
    query_unit, query_inverse = lane_units(query_lanes)
    key_unit, unused_inverse = lane_units(to_lanes(key_source[:, :, :C], length))
    value_lanes = to_lanes(key_source[:, :, C:], length)
    lane_pad = ((0, 0), (0, 0), (reach, reach))
    key_padded = jnp.pad(key_unit, lane_pad)
    value_padded = jnp.pad(value_lanes, lane_pad)
    inside_padded = jnp.pad(inside, (reach, reach))
    scales = head_scale[:, None]
    shifts = [
        (shift_row - RADIUS) * key_cols + (shift_col - RADIUS)
        for shift_row in range(span)
        for shift_col in range(span)
    ]
    exp_weights = []
    cosines = []
    weight_total = jnp.zeros((HEADS, length), jnp.float32)
    weighted_sum = jnp.zeros((HEADS, HEAD_DIM, length), jnp.float32)
    for shift in shifts:
        key_block = key_padded[:, :, reach + shift : reach + shift + length]
        value_block = value_padded[:, :, reach + shift : reach + shift + length]
        inside_block = inside_padded[reach + shift : reach + shift + length]
        cosine = jnp.sum(query_unit * key_block, axis=1)
        weight = jnp.exp(scales * cosine) * (inside_block * query_ok)[None, :]
        exp_weights.append(weight)
        cosines.append(cosine)
        weight_total = weight_total + weight
        weighted_sum = weighted_sum + weight[:, None, :] * value_block
    safe_total = jnp.where(query_ok[None, :] > 0, weight_total, 1.0)
    attended = weighted_sum / safe_total[:, None, :]
    attended_pixels = attended.reshape(C, length).T.reshape(key_rows, key_cols, C)
    mixed = attended_pixels[margin : margin + TH, margin : margin + TW].astype(jnp.bfloat16)
    output = (image_float + jnp.dot(mixed, w_out, preferred_element_type=jnp.float32)).astype(
        jnp.bfloat16
    )
    grad_flat = jnp.pad(cotangent, border).reshape(length, C)
    grad_mixed = lax.dot_general(
        w_out, grad_flat, (((1,), (1,)), ((), ())), preferred_element_type=jnp.float32
    ).reshape(HEADS, HEAD_DIM, length)
    out_term = jnp.dot(
        mixed.reshape(-1, C).T, cotangent.reshape(-1, C), preferred_element_type=jnp.float32
    )
    row_dot = jnp.sum(grad_mixed * attended, axis=1)
    grad_query_unit = jnp.zeros((HEADS, HEAD_DIM, length), jnp.float32)
    scale_term = jnp.zeros((HEADS,), jnp.float32)
    attentions = []
    grad_cosines = []
    for offset_index, shift in enumerate(shifts):
        key_block = key_padded[:, :, reach + shift : reach + shift + length]
        value_block = value_padded[:, :, reach + shift : reach + shift + length]
        attention = exp_weights[offset_index] / safe_total
        grad_attention = jnp.sum(grad_mixed * value_block, axis=1)
        grad_score = attention * (grad_attention - row_dot)
        scale_term = scale_term + jnp.sum(
            grad_score * cosines[offset_index] * own_ok[None, :], axis=1
        )
        grad_cosine = grad_score * scales
        grad_query_unit = grad_query_unit + grad_cosine[:, None, :] * key_block
        attentions.append(jnp.pad(attention, ((0, 0), (reach, reach))))
        grad_cosines.append(jnp.pad(grad_cosine, ((0, 0), (reach, reach))))
    query_padded = jnp.pad(query_unit, lane_pad)
    grad_padded = jnp.pad(grad_mixed, lane_pad)
    grad_keys = jnp.zeros((HEADS, HEAD_DIM, length), jnp.float32)
    grad_values = jnp.zeros((HEADS, HEAD_DIM, length), jnp.float32)
    for offset_index, shift in enumerate(shifts):
        back = reach - shift
        cosine_back = grad_cosines[offset_index][:, back : back + length]
        attention_back = attentions[offset_index][:, back : back + length]
        grad_keys = grad_keys + cosine_back[:, None, :] * query_padded[:, :, back : back + length]
        grad_values = (
            grad_values + attention_back[:, None, :] * grad_padded[:, :, back : back + length]
        )
    rim_grads = jnp.concatenate(
        [grad_keys.reshape(C, length), grad_values.reshape(C, length)], axis=0
    ).T.reshape(key_rows, key_cols, 2 * C)
    extended = padded(rim_grads.astype(jnp.bfloat16), (("row", 0), ("col", 1)), RADIUS).astype(
        rim_grads.dtype
    )
    folded = extended[2 * RADIUS : 2 * RADIUS + TH]
    folded = folded.at[:RADIUS].add(extended[:RADIUS])
    folded = folded.at[TH - RADIUS :].add(extended[TH + 3 * RADIUS :])
    collected = folded[:, 2 * RADIUS : 2 * RADIUS + TW]
    collected = collected.at[:, :RADIUS].add(folded[:, :RADIUS])
    collected = collected.at[:, TW - RADIUS :].add(folded[:, TW + 3 * RADIUS :])
    grad_key_unit = collected[:, :, :C].reshape(TH, TW, HEADS, HEAD_DIM)
    own_key_unit, own_key_inverse = unit_parts(
        key_source[margin : margin + TH, margin : margin + TW, :C].astype(jnp.float32)
    )
    grad_key = unit_backward(own_key_unit, own_key_inverse, grad_key_unit)
    along = jnp.sum(query_unit * grad_query_unit, axis=1, keepdims=True)
    grad_query_lanes = (grad_query_unit - query_unit * along) * query_inverse
    grad_query_pixels = grad_query_lanes.reshape(C, length).T.reshape(key_rows, key_cols, C)
    grad_query = grad_query_pixels[margin : margin + TH, margin : margin + TW]
    grad_packed = jnp.concatenate(
        [grad_query, grad_key.reshape(TH, TW, C), collected[:, :, C:]], axis=-1
    ).astype(jnp.bfloat16)
    qkv_term = jnp.dot(
        normed.reshape(-1, C).T, grad_packed.reshape(-1, 3 * C), preferred_element_type=jnp.float32
    )
    grad_normed = jnp.dot(grad_packed, w_qkv.T, preferred_element_type=jnp.float32)
    normed_value, norm_pull = jax.vjp(rms_norm, image_float, norm_gain)
    grad_image_norm, gain_term = norm_pull(grad_normed)
    grad_image = (cotangent.astype(jnp.float32) + grad_image_norm).astype(jnp.bfloat16)
    factor = 1.0 / math.sqrt(height * breadth)
    qkv_total, out_total, gain_total, scale_total = lax.psum(
        (qkv_term, out_term, gain_term, scale_term), ("row", "col")
    )
    return (
        output,
        grad_image,
        qkv_total * factor,
        out_total * factor,
        gain_total * factor,
        scale_total * factor,
    )


def solution(mesh):
    placed = (P("row", "col", None), P(), P(), P(), P(), P("row", "col", None))
    return jax.shard_map(
        on_device,
        mesh=mesh,
        in_specs=placed,
        out_specs=(P("row", "col", None), P("row", "col", None), P(), P(), P(), P()),
        check_vma=False,
    )
```

profile of v0, /device:TPU:1, one launch (start us, length us, event | category | flops | bytes accessed | tf_op | source)
XLA Modules:
  0.0 717.6 jit_solution(13579197847423389263)
XLA Ops:
  9.4 3.9 collective-permute-start
  13.3 1.4 collective-permute-start.1
  20.6 4.0 collective-permute-start.2
  24.7 3.4 collective-permute-start.3
  30.7 2.0 multiply_reduce_fusion.96
  32.8 2.7 multiply_reduce_fusion.98
  35.5 2.7 multiply_reduce_fusion.97
  38.8 2.1 multiply_reduce_fusion.49
  40.9 2.1 multiply_reduce_fusion.47
  43.4 1.6 add_select_fusion
  45.3 6.9 multiply_reduce_fusion.24
  77.0 11.9 %fusion.5 = bf16[4,64,308]{2,1,0:T(8,128)(2,1)S(1)} fusion(f32[4,64,308]{2,1,0:T(8,128)S(1)} %get-tuple-element.320, f32[4,308]{1,0:T(4,128)S(1)} %copy-done.74, f32[4,308]{1,0:T(4,128)} %copy-done.106, f32[4,308]{1,0:T(4,128)} %copy-done.91, f32[4,308]{1,0:T(4,128)} %copy-done.90, f32[4,308]{1,0:T(4,128)} %copy-done.89, f32[4,308]{1,0:T(4,128)} %copy-done.88, ...), kind=kOutput, calls=%fused_computation.199 | output fusion | flops 15692047 | bytes 2338816 | tf_op jit(solution)/shard_map/mul | solution.py:197
  89.0 6.5 fusion.102
  95.5 6.6 fusion.198
  102.8 4.3 collective-permute-start.4
  107.3 1.3 collective-permute-start.5
  111.1 2.3 collective-permute-done.5
  113.5 3.1 collective-permute-start.6
  116.6 1.9 collective-permute-start.7
  119.7 2.7 collective-permute-done.7
  124.9 1.2 convolution_bitcast_fusion
  126.2 119.7 %all-reduce.103 = (f32[256]{0:T(256)S(1)}, f32[4]{0:T(128)S(1)}) all-reduce(f32[256]{0:T(256)S(1)} %get-tuple-element.165, f32[4]{0:T(128)S(1)} %add_add_fusion.1), channel_id=1, replica_groups=mesh['row'=32,'col'=16] {'row','col'}, use_global_device_ids=true, to_apply=%region_109.110 | all-reduce | flops 260 | bytes 2080 | tf_op jit(solution)/shard_map/psum | solution.py:211
  247.7 460.2 %all-reduce.107.cloned.1.call-done = (f32[256,768]{1,0:T(8,128)}, f32[256,256]{1,0:T(8,128)}) async-done(((f32[256,768]{1,0:T(8,128)}, f32[256,256]{1,0:T(8,128)}), (f32[256,768]{1,0:T(8,128)}, f32[256,256]{1,0:T(8,128)})) %all-reduce.107.cloned.1.call-update) | async-done | bytes 1048592 | tf_op jit(solution)/shard_map/psum | solution.py:211
  707.9 2.1 broadcast_multiply_fusion
  (450 shorter events, 44.0 us)
Async XLA Ops:
  7.2 700.7 %all-reduce.107.cloned.1.call-start = ((), (), s32[]{:S(2)}) async-start(), calls=%async_computation | async-start | bytes 2097152 | tf_op jit(solution)/shard_map/psum | solution.py:211
  9.4 11.2 %collective-permute-start = (bf16[3,16,512]{2,1,0:T(8,128)(2,1)S(1)}, bf16[3,16,512]{2,1,0:T(8,128)(2,1)S(1)}, u32[]{:S(2)}, u32[]{:S(2)}) collective-permute-start(bf16[3,16,512]{2,1,0:T(8,128)(2,1)S(1)} %get-tuple-element.331), channel_id=1, source_target_pairs={{0,16},{16,32},{32,48},{48,64},{64,80},{80,96},{96,112},{112,128},... | collective-permute-start | bytes 147464 | tf_op jit(solution)/shard_map/ppermute | solution.py:28
  13.3 7.3 %collective-permute-start.1 = (bf16[3,16,512]{2,1,0:T(8,128)(2,1)S(1)}, bf16[3,16,512]{2,1,0:T(8,128)(2,1)S(1)}, u32[]{:S(2)}, u32[]{:S(2)}) collective-permute-start(bf16[3,16,512]{2,1,0:T(8,128)(2,1)S(1)} %get-tuple-element.332), channel_id=1, source_target_pairs={{16,0},{32,16},{48,32},{64,48},{80,64},{96,80},{112,96},{128,112},... | collective-permute-start | bytes 147464 | tf_op jit(solution)/shard_map/ppermute | solution.py:30
  20.6 8.5 %collective-permute-start.2 = (bf16[14,3,512]{2,1,0:T(4,128)(2,1)S(1)}, bf16[14,3,512]{2,1,0:T(4,128)(2,1)S(1)}, u32[]{:S(2)}, u32[]{:S(2)}) collective-permute-start(bf16[14,3,512]{2,1,0:T(4,128)(2,1)S(1)} %get-tuple-element.327), channel_id=1, source_target_pairs={{0,1},{1,2},{2,3},{3,4},{4,5},{5,6},{6,7},{7,8},{8,9},{9,10},{10,1... | collective-permute-start | bytes 129032 | tf_op jit(solution)/shard_map/ppermute | solution.py:28
  24.7 5.5 collective-permute-start.3
  56.0 20.9 %copy-start.74 = (f32[4,308]{1,0:T(4,128)S(1)}, f32[4,308]{1,0:T(4,128)}, u32[]{:S(2)}) copy-start(f32[4,308]{1,0:T(4,128)} %copy-done.73) | copy-start | bytes 14788
  57.2 19.7 %copy-start.83 = (f32[4,308]{1,0:T(4,128)}, f32[4,308]{1,0:T(4,128)S(1)}, u32[]{:S(2)}) copy-start(f32[4,308]{1,0:T(4,128)S(1)} %get-tuple-element.364) | copy-start | bytes 14788
  60.8 16.0 %copy-start.84 = (f32[4,308]{1,0:T(4,128)}, f32[4,308]{1,0:T(4,128)S(1)}, u32[]{:S(2)}) copy-start(f32[4,308]{1,0:T(4,128)S(1)} %get-tuple-element.373) | copy-start | bytes 14788
  60.8 16.0 %copy-start.85 = (f32[4,308]{1,0:T(4,128)}, f32[4,308]{1,0:T(4,128)S(1)}, u32[]{:S(2)}) copy-start(f32[4,308]{1,0:T(4,128)S(1)} %get-tuple-element.374) | copy-start | bytes 14788
  60.8 16.0 %copy-start.86 = (f32[4,308]{1,0:T(4,128)}, f32[4,308]{1,0:T(4,128)S(1)}, u32[]{:S(2)}) copy-start(f32[4,308]{1,0:T(4,128)S(1)} %get-tuple-element.375) | copy-start | bytes 14788
  60.9 16.0 %copy-start.87 = (f32[4,308]{1,0:T(4,128)}, f32[4,308]{1,0:T(4,128)S(1)}, u32[]{:S(2)}) copy-start(f32[4,308]{1,0:T(4,128)S(1)} %get-tuple-element.376) | copy-start | bytes 14788
  76.9 18.5 %copy-start.75 = (f32[4,308]{1,0:T(4,128)S(1)}, f32[4,308]{1,0:T(4,128)}, u32[]{:S(2)}) copy-start(f32[4,308]{1,0:T(4,128)} %get-tuple-element.445) | copy-start | bytes 14788
  76.9 18.5 %copy-start.76 = (f32[4,308]{1,0:T(4,128)S(1)}, f32[4,308]{1,0:T(4,128)}, u32[]{:S(2)}) copy-start(f32[4,308]{1,0:T(4,128)} %get-tuple-element.446) | copy-start | bytes 14788
  76.9 18.5 %copy-start.77 = (f32[4,308]{1,0:T(4,128)S(1)}, f32[4,308]{1,0:T(4,128)}, u32[]{:S(2)}) copy-start(f32[4,308]{1,0:T(4,128)} %get-tuple-element.443) | copy-start | bytes 14788
  77.0 18.5 %copy-start.78 = (f32[4,308]{1,0:T(4,128)S(1)}, f32[4,308]{1,0:T(4,128)}, u32[]{:S(2)}) copy-start(f32[4,308]{1,0:T(4,128)} %get-tuple-element.444) | copy-start | bytes 14788
  77.0 18.5 %copy-start.79 = (f32[4,308]{1,0:T(4,128)S(1)}, f32[4,308]{1,0:T(4,128)}, u32[]{:S(2)}) copy-start(f32[4,308]{1,0:T(4,128)} %get-tuple-element.441) | copy-start | bytes 14788
  77.0 18.5 %copy-start.80 = (f32[4,308]{1,0:T(4,128)S(1)}, f32[4,308]{1,0:T(4,128)}, u32[]{:S(2)}) copy-start(f32[4,308]{1,0:T(4,128)} %get-tuple-element.442) | copy-start | bytes 14788
  77.0 18.5 %copy-start.81 = (f32[4,308]{1,0:T(4,128)S(1)}, f32[4,308]{1,0:T(4,128)}, u32[]{:S(2)}) copy-start(f32[4,308]{1,0:T(4,128)} %get-tuple-element.497) | copy-start | bytes 14788
  77.0 18.5 %copy-start.82 = (f32[4,308]{1,0:T(4,128)S(1)}, f32[4,308]{1,0:T(4,128)}, u32[]{:S(2)}) copy-start(f32[4,308]{1,0:T(4,128)} %get-tuple-element.498) | copy-start | bytes 14788
  102.8 8.2 %collective-permute-start.4 = (bf16[3,22,512]{2,1,0:T(8,128)(2,1)S(1)}, bf16[3,22,512]{2,1,0:T(8,128)(2,1)S(1)}, u32[]{:S(2)}, u32[]{:S(2)}) collective-permute-start(bf16[3,22,512]{2,1,0:T(8,128)(2,1)S(1)} %slice.1639), channel_id=1, source_target_pairs={{0,16},{16,32},{32,48},{48,64},{64,80},{80,96},{96,112},{112,128},... | collective-permute-start | bytes 202760 | tf_op jit(solution)/shard_map/ppermute | solution.py:28
  107.3 6.2 collective-permute-start.5
  113.5 6.2 collective-permute-start.6
  116.6 5.8 collective-permute-start.7
  124.9 122.1 %copy-start.71 = (f32[8,16]{1,0:T(8,128)S(1)}, f32[8,16]{1,0:T(8,128)}, u32[]{:S(2)}) copy-start(f32[8,16]{1,0:T(8,128)} %copy-done.70) | copy-start | bytes 1540
  (132 other events, 914.7 us)
Sparse Core Ops, SparseCore 0:
  246.6 461.3 all-reduce.106
where the time goes:
time: 718 us
  waiting for transfers between devices  466 us (65%)
  blocking collectives  120 us (17%)
  other arithmetic  66.9 us (9%)
  starting transfers between devices  23.4 us (3%)
  local copies, waits for them, and re-layouts  19.9 us (3%)
  between operations  16.8 us (2%)
    psum x1, waiting for transfers between devices, on_device(): lax.psum((qkv_term, out_term, gain_term, scale_term), ('row', 'col'))  460 us
    psum x1, blocking collectives, on_device(): lax.psum((qkv_term, out_term, gain_term, scale_term), ('row', 'col'))  120 us
    ppermute x4, starting transfers between devices, padded(): lax.ppermute(tail, axis, [(i, (i + 1) % count) for i in range(ends)])  15.4 us
  transfers between devices with their start and end apart: 9, of which 4 were waited for; matrix products, arithmetic and copies ran while one was open for 2% of the time, Pallas kernels for 0%

commit v1 on v0

v1 whole, which is shorter than its diff:
```python
import math

import jax
import jax.numpy as jnp
from jax import lax
from jax.experimental import pallas as pl
from jax.experimental.pallas import tpu as pltpu
from jax.sharding import PartitionSpec as P

C = 256
HEADS = 4
HEAD_DIM = 64
RADIUS = 3
TH = 8
TW = 16
OWN = TH * TW
HALO = 224
KEYS = OWN + HALO
LANES = HEADS * OWN
EPS = 1e-06
NP = 16
NZ = 16
MESH = pl.DeviceIdType.MESH
F32 = jnp.float32
BF16 = jnp.bfloat16

PLACES = (
    (0, 48, -3, 0, 16),
    (48, 48, TH, 0, 16),
    (96, 32, 0, -3, 4),
    (128, 32, 0, TW, 4),
    (160, 16, -3, -3, 4),
    (176, 16, -3, TW, 4),
    (192, 16, TH, -3, 4),
    (208, 16, TH, TW, 4),
)
OWNERS = ((-1, 0), (1, 0), (0, -1), (0, 1), (-1, -1), (-1, 1), (1, -1), (1, 1))


def dot(a, b, contract=((1,), (0,))):
    return lax.dot_general(a, b, (contract, ((), ())), preferred_element_type=F32)


def key_mask(row, col, height, breadth):
    blocks = []
    for first, count, y0, x0, across in ((-1, OWN, 0, 0, TW),) + PLACES:
        place = lax.broadcasted_iota(jnp.int32, (count, OWN), 0)
        query = lax.broadcasted_iota(jnp.int32, (count, OWN), 1)
        y = place // across + y0
        x = place % across + x0
        ok = (jnp.abs(y - query // TW) <= RADIUS) & (jnp.abs(x - query % TW) <= RADIUS)
        gy = y + row * TH
        gx = x + col * TW
        ok = ok & (gy >= 0) & (gy < height) & (gx >= 0) & (gx < breadth)
        if across == 4:
            ok = ok & (place % 4 < RADIUS)
            if count == 16:
                ok = ok & (place // 4 < RADIUS)
        blocks.append(jnp.where(ok, 1.0, 0.0).astype(F32))
    return jnp.concatenate(blocks, axis=0)


def selection():
    blocks = []
    for first, count, y0, x0, across in PLACES[2:]:
        place = lax.broadcasted_iota(jnp.int32, (count, OWN), 0)
        pixel = lax.broadcasted_iota(jnp.int32, (count, OWN), 1)
        y = place // 4 + (y0 + TH) % TH
        x = place % 4 + (x0 + TW) % TW
        ok = (pixel == y * TW + x) & (place % 4 < RADIUS)
        if count == 16:
            ok = ok & (place // 4 < RADIUS)
        blocks.append(jnp.where(ok, 1.0, 0.0).astype(F32))
    return jnp.concatenate(blocks, axis=0).astype(BF16)


def block(
    rows,
    cols,
    factor,
    image_ref,
    w_qkv_ref,
    w_out_ref,
    gain_ref,
    scale_ref,
    cot_ref,
    output_ref,
    grad_image_ref,
    grad_qkv_ref,
    grad_out_ref,
    grad_gain_ref,
    grad_scale_ref,
    halo,
    side,
    grad_send,
    grad_back,
    q_block,
    g_block,
    total,
    send0,
    recv0,
    mine,
    small0,
    small0r,
    small1,
    send1,
    recv1,
    send2,
    recv2,
    recv3,
    gathered,
    sems,
):
    row = lax.axis_index("row")
    col = lax.axis_index("col")
    z = row // 2
    core = col % 2
    chip = (row % 2) * 8 + col // 2
    sibling = (row, col + 1 - 2 * core)

    def chip_id(other):
        return (z * 2 + other // 8, (other % 8) * 2 + core)

    def z_id(other):
        return (other * 2 + row % 2, col)

    def neighbour(step):
        return (lax.rem(row + step[0] + rows, rows), lax.rem(col + step[1] + cols, cols))

    barrier = pltpu.get_barrier_semaphore()
    for step in OWNERS:
        pl.semaphore_signal(barrier, inc=1, device_id=neighbour(step), device_id_type=MESH)
    pl.semaphore_signal(barrier, inc=1, device_id=sibling, device_id_type=MESH)

    def greet(k, carry):
        pl.semaphore_signal(
            barrier, inc=1, device_id=chip_id(lax.rem(chip + k, NP)), device_id_type=MESH
        )
        pl.semaphore_signal(
            barrier, inc=1, device_id=z_id(lax.rem(z + k, NZ)), device_id_type=MESH
        )
        return carry

    lax.fori_loop(1, NP, greet, 0)

    def remote(src, dst, sem, device):
        return pltpu.make_async_remote_copy(
            src_ref=src,
            dst_ref=dst,
            send_sem=sems.at[2 * sem],
            recv_sem=sems.at[2 * sem + 1],
            device_id=device,
            device_id_type=MESH,
        )

    def wait_sent(ref, sem):
        pltpu.make_async_copy(ref, ref, sems.at[2 * sem]).wait()

    def wait_received(ref, sem):
        pltpu.make_async_copy(ref, ref, sems.at[2 * sem + 1]).wait()

    sel = selection()
    side[...] = dot(sel, image_ref[...]).astype(BF16)

    pl.semaphore_wait(barrier, 8 + 1 + (NP - 1) + (NZ - 1))

    for place, step in zip(PLACES, OWNERS):
        first, count = place[0], place[1]
        if first == 0:
            src = image_ref.at[pl.ds(OWN - 48, 48)]
        elif first == 48:
            src = image_ref.at[pl.ds(0, 48)]
        else:
            src = side.at[pl.ds(first - 96, count)]
        remote(
            src, halo.at[pl.ds(first, count)], 0, neighbour((-step[0], -step[1]))
        ).start()

    gain = gain_ref[...]
    w_q = w_qkv_ref[:, :C]
    w_kv = w_qkv_ref[:, C:]
    cot = cot_ref[...]
    mask = key_mask(row, col, rows * TH, cols * TW)

    def norm(values):
        inverse = lax.rsqrt(jnp.mean(values * values, axis=-1, keepdims=True) + EPS)
        return inverse, (values * inverse * gain).astype(BF16)

    own_float = image_ref[...].astype(F32)
    own_inverse, own_normed = norm(own_float)
    own_normed_t = own_normed.astype(F32).T.astype(BF16)
    query = dot(own_normed, w_q).astype(BF16)
    query_t = query.astype(F32).T
    q_block[...] = jnp.zeros_like(q_block)
    g_block[...] = jnp.zeros_like(g_block)
    grad_mixed_t = dot(w_out_ref[...], cot, ((1,), (1,)))
    q_inverse = []
    for h in range(HEADS):
        ch = slice(h * HEAD_DIM, (h + 1) * HEAD_DIM)
        ln = slice(h * OWN, (h + 1) * OWN)
        part = query_t[ch]
        q_block[ch, ln] = part.astype(BF16)
        g_block[ch, ln] = grad_mixed_t[ch].astype(BF16)
        q_inverse.append(lax.rsqrt(jnp.sum(part * part, axis=0, keepdims=True) + EPS))
    own_kv = dot(own_normed, w_kv)

    wait_sent(halo, 0)
    wait_received(halo, 0)

    halo_float = halo[...].astype(F32)
    halo_inverse, halo_normed = norm(halo_float)
    halo_normed_t = halo_normed.astype(F32).T.astype(BF16)
    halo_kv = dot(halo_normed, w_kv)
    kv = jnp.concatenate([own_kv, halo_kv], axis=0).astype(BF16)
    keys = kv[:, :C]
    values = kv[:, C:]
    keys_float = keys.astype(F32)
    keys_t = keys_float.T.astype(BF16)
    values_t = values.astype(F32).T.astype(BF16)

    scores = dot(keys, q_block[...])
    grad_probs = dot(values, g_block[...])
    probs = []
    grad_logits = []
    k_inverse = []
    k_along = []
    attended_t = []
    grad_q_t = []
    scale_sum = jnp.zeros((1, OWN), F32)
    lane = lax.broadcasted_iota(jnp.int32, (1, OWN), 1)
    for h in range(HEADS):
        ch = slice(h * HEAD_DIM, (h + 1) * HEAD_DIM)
        ln = slice(h * OWN, (h + 1) * OWN)
        k_part = keys_float[:, ch]
        k_inv = lax.rsqrt(jnp.sum(k_part * k_part, axis=1, keepdims=True) + EPS)
        scale = scale_ref[h]
        logit = scores[:, ln] * k_inv * (q_inverse[h] * scale)
        weight = jnp.exp(logit) * mask
        prob = weight * (1.0 / jnp.sum(weight, axis=0, keepdims=True))
        prob_bf = prob.astype(BF16)
        probs.append(prob_bf)
        attended_t.append(dot(values_t[ch], prob_bf))
        grad_prob = grad_probs[:, ln]
        row_dot = jnp.sum(prob * grad_prob, axis=0, keepdims=True)
        grad_logit = prob * (grad_prob - row_dot)
        product = grad_logit * logit
        along_q = jnp.sum(product, axis=0, keepdims=True)
        scale_sum = scale_sum + jnp.where(
            lane == h, jnp.sum(along_q, axis=1, keepdims=True) / scale, 0.0
        )
        k_along.append(jnp.sum(product, axis=1, keepdims=True))
        k_inverse.append(k_inv)
        grad_cos = grad_logit * scale
        grad_logits.append((grad_cos * q_inverse[h]).astype(BF16))
        unit_grad = dot(keys_t[ch], (grad_cos * k_inv).astype(BF16))
        grad_q_t.append(
            q_inverse[h] * (unit_grad - query_t[ch] * (q_inverse[h] * along_q))
        )

    attended_t = jnp.concatenate(attended_t, axis=0)
    mixed_t = attended_t.astype(BF16)
    mixed = attended_t.T.astype(BF16)
    output_ref[...] = (own_float + dot(mixed, w_out_ref[...])).astype(BF16)
    total[pl.ds(3 * C, C), :] = dot(mixed_t, cot)

    grad_q = jnp.concatenate(grad_q_t, axis=0).T.astype(BF16)
    grad_k_unit = dot(jnp.concatenate(grad_logits, axis=1), q_block[...], ((1,), (1,)))
    grad_v = dot(jnp.concatenate(probs, axis=1), g_block[...], ((1,), (1,))).astype(BF16)
    low = lax.broadcasted_iota(jnp.int32, (1, OWN), 1) < HEAD_DIM
    grad_k = []
    for t in range(2):
        ln = slice(t * OWN, (t + 1) * OWN)
        inv = jnp.where(low, k_inverse[2 * t], k_inverse[2 * t + 1])
        along = jnp.where(low, k_along[2 * t], k_along[2 * t + 1])
        grad_k.append(inv * (grad_k_unit[:, ln] - keys_float[:, ln] * (inv * along)))
    grad_k = jnp.concatenate(grad_k, axis=1).astype(BF16)
    grad_kv = jnp.concatenate([grad_k, grad_v], axis=1)

    total[pl.ds(0, C), :] = dot(own_normed_t, grad_q)
    normed_t = jnp.concatenate([own_normed_t, halo_normed_t], axis=1)
    kv_term = dot(normed_t, grad_kv)
    total[pl.ds(C, C), :] = kv_term[:, :C]
    total[pl.ds(2 * C, C), :] = kv_term[:, C:]

    half = pl.multiple_of((1 - core) * 512, 512)
    kept = pl.multiple_of(core * 512, 512)
    send0[...] = total[pl.ds(half, 512), :].astype(BF16)
    remote(send0, recv0, 1, sibling).start()

    grad_normed = dot(grad_kv, w_kv, ((1,), (1,)))
    grad_normed_own = grad_normed[:OWN] + dot(grad_q, w_q, ((1,), (1,)))

    def norm_back(values, inverse, grad):
        scaled = values * inverse
        gain_term = jnp.sum(grad * scaled, axis=0, keepdims=True)
        grad = grad * gain
        along = jnp.mean(grad * scaled, axis=-1, keepdims=True)
        return gain_term, inverse * (grad - scaled * along)

    gain_own, image_own = norm_back(own_float, own_inverse, grad_normed_own)
    gain_halo, image_halo = norm_back(halo_float, halo_inverse, grad_normed[OWN:])
    gain_sum = gain_own + gain_halo
    grad_send[...] = image_halo.astype(BF16)
    for place, step in zip(PLACES, OWNERS):
        there = pl.ds(place[0], place[1])
        remote(grad_send.at[there], grad_back.at[there], 2, neighbour(step)).start()

    small0[...] = jnp.concatenate(
        [scale_sum, gain_sum[:, :OWN], gain_sum[:, OWN:], jnp.zeros((5, OWN), F32)], axis=0
    )
    remote(small0, small0r, 3, sibling).start()

    wait_received(recv0, 1)
    mine[...] = total[pl.ds(kept, 512), :] + recv0[...].astype(F32)
    send1[...] = mine[...].astype(BF16)

    def chunk(other):
        return pl.ds(pl.multiple_of(other * 32, 32), 32)

    def scatter1(k, carry):
        other = lax.rem(chip + k, NP)
        remote(send1.at[chunk(other)], recv1.at[chunk(k - 1)], 4, chip_id(other)).start()
        return carry

    lax.fori_loop(1, NP, scatter1, 0)
    wait_received(small0r, 3)
    small1[chip] = small0[...] + small0r[...]

    def scatter1s(k, carry):
        other = lax.rem(chip + k, NP)
        remote(small1.at[chip], small1.at[chip], 5, chip_id(other)).start()
        return carry

    lax.fori_loop(1, NP, scatter1s, 0)

    wait_received(grad_back, 2)
    grad_image = cot.astype(F32) + image_own
    grad_image = grad_image + dot(sel, grad_back[pl.ds(96, 128), :], ((0,), (0,)))
    top = grad_back[pl.ds(48, 48), :].astype(F32)
    bottom = grad_back[pl.ds(0, 48), :].astype(F32)
    grad_image = jnp.concatenate(
        [grad_image[:48] + top, grad_image[48:80], grad_image[80:] + bottom], axis=0
    )
    grad_image_ref[...] = grad_image.astype(BF16)

    wait_received(recv1.at[pl.ds(0, 15 * 32)], 4)
    summed = mine[chunk(chip), :]
    for k in range(NP - 1):
        summed = summed + recv1[pl.ds(k * 32, 32), :].astype(F32)
    wait_received(small1.at[pl.ds(0, 15)], 5)
    small = small1[0]
    for k in range(1, NP):
        small = small + small1[k]

    for i in range(NZ):
        a, b, c = i // 4, (i // 2) % 2, i % 2
        send2[i] = jnp.concatenate(
            [summed[8 * a + 4 * c : 8 * a + 4 * c + 4, 128 * b : 128 * b + 128], small[:4]],
            axis=0,
        )
    recv2[z] = send2[z]

    def scatter2(k, carry):
        other = lax.rem(z + k, NZ)
        remote(send2.at[other], recv2.at[z], 6, z_id(other)).start()
        return carry

    lax.fori_loop(1, NZ, scatter2, 0)
    wait_received(recv2.at[pl.ds(0, 15)], 6)
    piece = recv2[0]
    for k in range(1, NZ):
        piece = piece + recv2[k]
    piece = piece * factor
    grad_scale_ref[...] = piece[4:5]
    grad_gain_ref[...] = jnp.concatenate([piece[5:6], piece[6:7]], axis=1)
    recv3[z] = piece

    def gather3(k, carry):
        other = lax.rem(z + k, NZ)
        remote(recv3.at[z], recv3.at[z], 7, z_id(other)).start()
        return carry

    lax.fori_loop(1, NZ, gather3, 0)
    wait_received(recv3.at[pl.ds(0, 15)], 7)
    lines = []
    for a in range(4):
        lines.append(
            jnp.concatenate(
                [
                    jnp.concatenate([recv3[4 * a + 2 * b + c, :4] for c in range(2)], axis=0)
                    for b in range(2)
                ],
                axis=1,
            )
        )
    here = pl.multiple_of(core * 512 + chip * 32, 32)
    gathered[pl.ds(here, 32), :] = jnp.concatenate(lines, axis=0).astype(BF16)

    def gather4(k, carry):
        other = lax.rem(chip + k, NP)
        spot = gathered.at[pl.ds(here, 32)]
        remote(spot, spot, 8, chip_id(other)).start()
        return carry

    lax.fori_loop(1, NP, gather4, 0)
    wait_received(gathered.at[pl.ds(0, 15 * 32)], 8)
    mine_half = gathered.at[pl.ds(kept, 512)]
    remote(mine_half, mine_half, 9, sibling).start()
    wait_received(mine_half, 9)

    for j in range(3):
        grad_qkv_ref[:, pl.ds(j * C, C)] = gathered[pl.ds(j * C, C), :].astype(F32)
    grad_out_ref[...] = gathered[pl.ds(3 * C, C), :].astype(F32)

    wait_sent(send0, 1)
    wait_sent(grad_send, 2)
    wait_sent(small0, 3)
    wait_sent(recv1.at[pl.ds(0, 15 * 32)], 4)
    wait_sent(small1.at[pl.ds(0, 15)], 5)
    wait_sent(send2.at[pl.ds(0, 15)], 6)
    wait_sent(recv3.at[pl.ds(0, 15)], 7)
    wait_sent(gathered.at[pl.ds(0, 15 * 32)], 8)
    wait_sent(mine_half, 9)


def on_device(image, w_qkv, w_out, norm_gain, head_scale, cotangent):
    rows = lax.axis_size("row")
    cols = lax.axis_size("col")
    vmem = pl.BlockSpec(memory_space=pltpu.VMEM)
    smem = pl.BlockSpec(memory_space=pltpu.SMEM)
    factor = 1.0 / math.sqrt(rows * TH * cols * TW)

    def kernel(*refs):
        block(rows, cols, factor, *refs)

    output, grad_image, grad_qkv, grad_out, grad_gain, grad_scale = pl.pallas_call(
        kernel,
        out_shape=(
            jax.ShapeDtypeStruct((OWN, C), BF16),
            jax.ShapeDtypeStruct((OWN, C), BF16),
            jax.ShapeDtypeStruct((C, 3 * C), F32),
            jax.ShapeDtypeStruct((C, C), F32),
            jax.ShapeDtypeStruct((1, C), F32),
            jax.ShapeDtypeStruct((1, OWN), F32),
        ),
        in_specs=[vmem, vmem, vmem, vmem, smem, vmem],
        out_specs=(vmem,) * 6,
        scratch_shapes=[
            pltpu.VMEM((HALO, C), BF16),
            pltpu.VMEM((OWN, C), BF16),
            pltpu.VMEM((HALO, C), BF16),
            pltpu.VMEM((HALO, C), BF16),
            pltpu.VMEM((C, LANES), BF16),
            pltpu.VMEM((C, LANES), BF16),
            pltpu.VMEM((4 * C, C), F32),
            pltpu.VMEM((2 * C, C), BF16),
            pltpu.VMEM((2 * C, C), BF16),
            pltpu.VMEM((2 * C, C), F32),
            pltpu.VMEM((8, OWN), F32),
            pltpu.VMEM((8, OWN), F32),
            pltpu.VMEM((NP, 8, OWN), F32),
            pltpu.VMEM((2 * C, C), BF16),
            pltpu.VMEM((2 * C, C), BF16),
            pltpu.VMEM((NZ, 8, OWN), F32),
            pltpu.VMEM((NZ, 8, OWN), F32),
            pltpu.VMEM((NZ, 8, OWN), F32),
            pltpu.VMEM((4 * C, C), BF16),
            pltpu.SemaphoreType.DMA((20,)),
        ],
        compiler_params=pltpu.CompilerParams(
            collective_id=0, has_side_effects=True, vmem_limit_bytes=48 * 1024 * 1024
        ),
    )(
        image.reshape(OWN, C),
        w_qkv,
        w_out,
        norm_gain.reshape(1, C),
        head_scale,
        cotangent.reshape(OWN, C),
    )
    return (
        output.reshape(TH, TW, C),
        grad_image.reshape(TH, TW, C),
        grad_qkv,
        grad_out,
        grad_gain.reshape(C),
        grad_scale[0, :HEADS],
    )


def solution(mesh):
    placed = (P("row", "col", None), P(), P(), P(), P(), P("row", "col", None))
    return jax.shard_map(
        on_device,
        mesh=mesh,
        in_specs=placed,
        out_specs=(P("row", "col", None), P("row", "col", None), P(), P(), P(), P()),
        check_vma=False,
    )
```

time: 718 us -> 67.1 us (0.09)
  waiting for transfers between devices: 466 us -> 0 us
  blocking collectives: 120 us -> 0 us
  other arithmetic: 66.9 us -> 0 us
  Pallas kernels: 0 us -> 58 us
  starting transfers between devices: 23.4 us -> 0 us
  between operations: 16.8 us -> 0.67 us
  local copies, waits for them, and re-layouts: 19.9 us -> 8.16 us
    psum x1 -> x0, waiting for transfers between devices: 460 us -> none  [on_device(): lax.psum((qkv_term, out_term, gain_term, scale_term), ('row', 'col'))]
    psum x1 -> x0, blocking collectives: 120 us -> none  [on_device(): lax.psum((qkv_term, out_term, gain_term, scale_term), ('row', 'col'))]
    pallas_call x0 -> x1, Pallas kernels: none -> 58 us  [on_device(): pl.pallas_call(kernel, out_shape=(jax.ShapeDtypeStruct((OWN, C), BF16), j...]
    reduce_sum x20 -> x0, other arithmetic: 27.4 us -> none  [the longest x3 11.1 us: on_device(): grad_attention = jnp.sum(grad_mixed * value_block, axis=1)]
    ppermute x8 -> x0, starting transfers between devices: 23.4 us -> none  [the longest x4 15.4 us: padded(): lax.ppermute(tail, axis, [(i, (i + 1) % count) for i in range(ends)])]
    mul x20 -> x0, other arithmetic: 21.8 us -> none  [the longest x1 11.9 us: on_device(): grad_query_lanes = (grad_query_unit - query_unit * along) * query_inverse]
    slice x58 -> x0, local copies, waits for them, and re-layouts: 16 us -> none  [the longest x25 8.47 us: on_device(): cosine_back = grad_cosines[offset_index][:, back:back + length]]
    another operation x3 -> x0, other arithmetic: 13.1 us -> none
  transfers between devices with their start and end apart: 9 -> 0, of which waited for: 4 -> 0; matrix products, arithmetic and copies ran while one was open for 2% -> 0% of each run, Pallas kernels for 0% -> 0%
where the time goes in v1:
time: 67.1 us; the launch traced here: 66.8 us
  Pallas kernels  58 us (86%)
  local copies, waits for them, and re-layouts  8.16 us (12%)
    pallas_call x1, Pallas kernels, on_device(): pl.pallas_call(kernel, out_shape=(jax.ShapeDtypeStruct((OWN, C), BF16), j...  58 us
    unnamed x17, local copies, waits for them, and re-layouts  7.65 us

profile of v1, /device:TPU:1, one launch (start us, length us, event | category | flops | bytes accessed | tf_op | source)
XLA Modules:
  0.0 66.8 jit_solution(6618287045077093132)
XLA Ops:
  0.6 0.0 copy-start.4
  0.6 0.0 copy-start.5
  0.7 0.7 copy-done.4
  1.3 0.0 copy-done.5
  1.3 0.0 copy-start
  1.3 1.0 %copy-done = bf16[256,768]{1,0:T(8,128)(2,1)S(1)} copy-done((bf16[256,768]{1,0:T(8,128)(2,1)S(1)}, bf16[256,768]{1,0:T(8,128)(2,1)}, u32[]{:S(2)}) %copy-start) | copy-done | bytes 393240
  2.3 0.0 copy-start.1
  2.3 0.9 %copy-done.1 = bf16[256,256]{1,0:T(8,128)(2,1)S(1)} copy-done((bf16[256,256]{1,0:T(8,128)(2,1)S(1)}, bf16[256,256]{1,0:T(8,128)(2,1)}, u32[]{:S(2)}) %copy-start.1) | copy-done | bytes 131096
  3.2 0.0 copy-start.2
  3.2 0.8 %copy-done.2 = bf16[8,16,256]{2,1,0:T(8,128)(2,1)S(1)} copy-done((bf16[8,16,256]{2,1,0:T(8,128)(2,1)S(1)}, bf16[8,16,256]{2,1,0:T(8,128)(2,1)}, u32[]{:S(2)}) %copy-start.2) | copy-done | bytes 65560
  4.1 0.0 copy-start.3
  4.1 0.8 %copy-done.3 = bf16[8,16,256]{2,1,0:T(8,128)(2,1)S(1)} copy-done((bf16[8,16,256]{2,1,0:T(8,128)(2,1)S(1)}, bf16[8,16,256]{2,1,0:T(8,128)(2,1)}, u32[]{:S(2)}) %copy-start.3) | copy-done | bytes 65560
  4.9 58.0 %shard_map.109 = (bf16[128,256]{1,0:T(8,128)(2,1)S(1)}, bf16[128,256]{1,0:T(8,128)(2,1)S(1)}, f32[256,768]{1,0:T(8,128)S(1)}, f32[256,256]{1,0:T(8,128)S(1)}, f3...) custom-call(bf16[128,256]{1,0:T(8,128)(2,1)S(1)} %bitcast.8, bf16[256,768]{1,0:T(8,128)(2,1)S(1)} %copy-done, ...), custom_call_target="tpu_custom_call" | custom-call | tf_op jit(solution)/shard_map/pallas_call | solution.py:436
  62.9 0.5 slice_bitcast_fusion
  63.4 0.6 copy.17
  64.0 0.6 copy.18
  64.7 0.9 %copy.19 = f32[256,768]{1,0:T(8,128)} copy(f32[256,768]{1,0:T(8,128)S(1)} %get-tuple-element.26) | data formatting | bytes 1572864
  65.5 0.7 %copy.20 = f32[256,256]{1,0:T(8,128)} copy(f32[256,256]{1,0:T(8,128)S(1)} %get-tuple-element.27) | data formatting | bytes 524288
  66.2 0.6 copy.21
Async XLA Ops:
  0.6 0.7 %copy-start.4 = (f32[256]{0:T(256)S(1)}, f32[256]{0:T(256)}, u32[]{:S(2)}) copy-start(f32[256]{0:T(256)} %param.9) | copy-start | bytes 3076
  0.6 0.7 %copy-start.5 = (f32[4]{0:T(128)S(1)}, f32[4]{0:T(128)}, u32[]{:S(2)}) copy-start(f32[4]{0:T(128)} %refs_4_.1) | copy-start | bytes 52
  1.3 1.0 %copy-start = (bf16[256,768]{1,0:T(8,128)(2,1)S(1)}, bf16[256,768]{1,0:T(8,128)(2,1)}, u32[]{:S(2)}) copy-start(bf16[256,768]{1,0:T(8,128)(2,1)} %refs_1_.1) | copy-start | bytes 1179652
  2.3 0.9 %copy-start.1 = (bf16[256,256]{1,0:T(8,128)(2,1)S(1)}, bf16[256,256]{1,0:T(8,128)(2,1)}, u32[]{:S(2)}) copy-start(bf16[256,256]{1,0:T(8,128)(2,1)} %refs_2_.1) | copy-start | bytes 393220
  3.2 0.8 %copy-start.2 = (bf16[8,16,256]{2,1,0:T(8,128)(2,1)S(1)}, bf16[8,16,256]{2,1,0:T(8,128)(2,1)}, u32[]{:S(2)}) copy-start(bf16[8,16,256]{2,1,0:T(8,128)(2,1)} %param.6) | copy-start | bytes 196612
  4.1 0.8 %copy-start.3 = (bf16[8,16,256]{2,1,0:T(8,128)(2,1)S(1)}, bf16[8,16,256]{2,1,0:T(8,128)(2,1)}, u32[]{:S(2)}) copy-start(bf16[8,16,256]{2,1,0:T(8,128)(2,1)} %param.11) | copy-start | bytes 196612

commit v2 on v1

v2 whole, which is shorter than its diff:
```python
import math

import jax
import jax.numpy as jnp
from jax import lax
from jax.experimental import pallas as pl
from jax.experimental.pallas import tpu as pltpu
from jax.sharding import PartitionSpec as P

C = 256
HEADS = 4
HEAD_DIM = 64
RADIUS = 3
TH = 8
TW = 16
OWN = TH * TW
HALO = 224
KEYS = OWN + HALO
LANES = HEADS * OWN
EPS = 1e-06
NP = 16
VMEM_LIMIT = 60 * 1024 * 1024
NZ = 16
MESH = pl.DeviceIdType.MESH
F32 = jnp.float32
BF16 = jnp.bfloat16

PLACES = (
    (0, 48, -3, 0, 16),
    (48, 48, TH, 0, 16),
    (96, 32, 0, -3, 4),
    (128, 32, 0, TW, 4),
    (160, 16, -3, -3, 4),
    (176, 16, -3, TW, 4),
    (192, 16, TH, -3, 4),
    (208, 16, TH, TW, 4),
)
OWNERS = ((-1, 0), (1, 0), (0, -1), (0, 1), (-1, -1), (-1, 1), (1, -1), (1, 1))

STEPS = sorted(
    ((dx, dy) for dx in range(4) for dy in range(4) if dx or dy),
    key=lambda step: (-min(step[0], 4 - step[0]) - min(step[1], 4 - step[1]), step),
)
CAST_ORDER = (1, 2, 3, 4, 5, 15, 6, 14, 7, 13, 8, 12, 9, 11, 10)
HALO_SEM, BACK_SEM, SMALL_CORE, SMALL_PLANE, SMALL_LINE, SMALL_CAST, SMALL_GATHER = range(7)
CORE_SEM, PLANE_SEM, LINE_SEM, CAST_SEM, GATHER_SEM, BOTH_SEM = range(7, 19, 2)


def dot(a, b, contract=((1,), (0,))):
    return lax.dot_general(a, b, (contract, ((), ())), preferred_element_type=F32)


def key_mask(row, col, height, breadth):
    blocks = []
    for first, count, y0, x0, across in ((-1, OWN, 0, 0, TW),) + PLACES:
        place = lax.broadcasted_iota(jnp.int32, (count, OWN), 0)
        query = lax.broadcasted_iota(jnp.int32, (count, OWN), 1)
        y = place // across + y0
        x = place % across + x0
        ok = (jnp.abs(y - query // TW) <= RADIUS) & (jnp.abs(x - query % TW) <= RADIUS)
        gy = y + row * TH
        gx = x + col * TW
        ok = ok & (gy >= 0) & (gy < height) & (gx >= 0) & (gx < breadth)
        if across == 4:
            ok = ok & (place % 4 < RADIUS)
            if count == 16:
                ok = ok & (place // 4 < RADIUS)
        blocks.append(jnp.where(ok, 1.0, 0.0).astype(F32))
    return jnp.concatenate(blocks, axis=0)


def selection():
    blocks = []
    for first, count, y0, x0, across in PLACES[2:]:
        place = lax.broadcasted_iota(jnp.int32, (count, OWN), 0)
        pixel = lax.broadcasted_iota(jnp.int32, (count, OWN), 1)
        y = place // 4 + (y0 + TH) % TH
        x = place % 4 + (x0 + TW) % TW
        ok = (pixel == y * TW + x) & (place % 4 < RADIUS)
        if count == 16:
            ok = ok & (place // 4 < RADIUS)
        blocks.append(jnp.where(ok, 1.0, 0.0).astype(F32))
    return jnp.concatenate(blocks, axis=0).astype(BF16)


def block(rows, cols, factor, *refs):
    (
        image_hbm,
        w_qkv_hbm,
        w_out_hbm,
        gain_hbm,
        scale_ref,
        cot_hbm,
        output_hbm,
        grad_image_hbm,
        grad_qkv_hbm,
        grad_out_hbm,
        small_hbm,
        image_ref,
        w_qkv_ref,
        w_out_ref,
        gain_ref,
        cot_ref,
        halo,
        side,
        grad_send,
        grad_back,
        q_block,
        g_block,
        total,
        core_send,
        core_recv,
        mine,
        plane_send,
        plane_recv,
        line_send,
        line_recv,
        gathered,
        small_own,
        small_core,
        small_plane,
        small_line,
        small_total,
        output_ref,
        grad_image_ref,
        grad_qkv_ref,
        grad_out_ref,
        sems,
        local_sems,
    ) = refs
    row = lax.axis_index("row")
    col = lax.axis_index("col")
    z = row // 2
    core = col % 2
    x = (col // 8) * 2 + row % 2
    y = (col // 2) % 4
    chip = x * 4 + y
    sibling = (row, col + 1 - 2 * core)

    loads = []
    for i, (src, dst) in enumerate(
        (
            (image_hbm, image_ref),
            (w_qkv_hbm, w_qkv_ref),
            (cot_hbm, cot_ref),
            (w_out_hbm, w_out_ref),
            (gain_hbm, gain_ref),
        )
    ):
        load = pltpu.make_async_copy(src, dst, local_sems.at[i])
        load.start()
        loads.append(load)

    stores = []

    def store(src, dst):
        copy = pltpu.make_async_copy(src, dst, local_sems.at[len(loads) + len(stores)])
        copy.start()
        stores.append(copy)

    def chip_id(ox, oy):
        return (z * 2 + ox % 2, (ox // 2) * 8 + oy * 2 + core)

    def z_id(other):
        return (other * 2 + row % 2, col)

    def neighbour(step):
        return (lax.rem(row + step[0] + rows, rows), lax.rem(col + step[1] + cols, cols))

    peers = []
    for dx, dy in STEPS:
        ox, oy = lax.rem(x + dx, 4), lax.rem(y + dy, 4)
        peers.append((ox * 4 + oy, chip_id(ox, oy)))

    barrier = pltpu.get_barrier_semaphore()

    def greet(device):
        pl.semaphore_signal(barrier, inc=1, device_id=device, device_id_type=MESH)

    for step in OWNERS:
        greet(neighbour(step))
    for other, device in peers:
        greet(device)

    @pl.when(z != 0)
    def _():
        greet(z_id(0))

    @pl.when(z == 0)
    def _():
        for k in range(1, NZ):
            greet(z_id(k))

    def remote(src, dst, sem, device):
        return pltpu.make_async_remote_copy(
            src_ref=src,
            dst_ref=dst,
            send_sem=sems.at[2 * sem],
            recv_sem=sems.at[2 * sem + 1],
            device_id=device,
            device_id_type=MESH,
        )

    def wait_sent(ref, sem):
        pltpu.make_async_copy(ref, ref, sems.at[2 * sem]).wait()

    def wait_received(ref, sem):
        pltpu.make_async_copy(ref, ref, sems.at[2 * sem + 1]).wait()

    sel = selection()
    loads[0].wait()
    side[...] = dot(sel, image_ref[...]).astype(BF16)

    @pl.when(z != 0)
    def _():
        pl.semaphore_wait(barrier, 8 + (NP - 1) + 1)

    @pl.when(z == 0)
    def _():
        pl.semaphore_wait(barrier, 8 + (NP - 1) + (NZ - 1))

    for place, step in reversed(tuple(zip(PLACES, OWNERS))):
        first, count = place[0], place[1]
        if first == 0:
            src = image_ref.at[pl.ds(OWN - 48, 48)]
        elif first == 48:
            src = image_ref.at[pl.ds(0, 48)]
        else:
            src = side.at[pl.ds(first - 96, count)]
        remote(
            src, halo.at[pl.ds(first, count)], HALO_SEM, neighbour((-step[0], -step[1]))
        ).start()

    for load in loads[1:]:
        load.wait()
    gain = gain_ref[...]
    w_q = w_qkv_ref[:, :C]
    w_kv = w_qkv_ref[:, C:]
    cot = cot_ref[...]
    mask = key_mask(row, col, rows * TH, cols * TW)

    def norm(values):
        inverse = lax.rsqrt(jnp.mean(values * values, axis=-1, keepdims=True) + EPS)
        return inverse, (values * inverse * gain).astype(BF16)

    own_float = image_ref[...].astype(F32)
    own_inverse, own_normed = norm(own_float)
    own_normed_t = own_normed.astype(F32).T.astype(BF16)
    query = dot(own_normed, w_q).astype(BF16)
    query_t = query.astype(F32).T
    q_block[...] = jnp.zeros_like(q_block)
    g_block[...] = jnp.zeros_like(g_block)
    grad_mixed_t = dot(w_out_ref[...], cot, ((1,), (1,)))
    q_inverse = []
    for h in range(HEADS):
        ch = slice(h * HEAD_DIM, (h + 1) * HEAD_DIM)
        ln = slice(h * OWN, (h + 1) * OWN)
        part = query_t[ch]
        q_block[ch, ln] = part.astype(BF16)
        g_block[ch, ln] = grad_mixed_t[ch].astype(BF16)
        q_inverse.append(lax.rsqrt(jnp.sum(part * part, axis=0, keepdims=True) + EPS))
    own_kv = dot(own_normed, w_kv)

    wait_received(halo, HALO_SEM)

    halo_float = halo[...].astype(F32)
    halo_inverse, halo_normed = norm(halo_float)
    halo_normed_t = halo_normed.astype(F32).T.astype(BF16)
    halo_kv = dot(halo_normed, w_kv)
    kv = jnp.concatenate([own_kv, halo_kv], axis=0).astype(BF16)
    keys = kv[:, :C]
    values = kv[:, C:]
    keys_float = keys.astype(F32)
    values_t = values.astype(F32).T.astype(BF16)
    normed_t = jnp.concatenate([own_normed_t, halo_normed_t], axis=1)

    scores = dot(keys, q_block[...])
    probs = []
    probs_bf = []
    logits = []
    k_inverse = []
    attended_t = []
    for h in range(HEADS):
        ch = slice(h * HEAD_DIM, (h + 1) * HEAD_DIM)
        ln = slice(h * OWN, (h + 1) * OWN)
        k_part = keys_float[:, ch]
        k_inv = lax.rsqrt(jnp.sum(k_part * k_part, axis=1, keepdims=True) + EPS)
        logit = scores[:, ln] * k_inv * (q_inverse[h] * scale_ref[h])
        weight = jnp.exp(logit) * mask
        prob = weight * (1.0 / jnp.sum(weight, axis=0, keepdims=True))
        probs.append(prob)
        probs_bf.append(prob.astype(BF16))
        logits.append(logit)
        k_inverse.append(k_inv)
        attended_t.append(dot(values_t[ch], probs_bf[h]))
    attended_t = jnp.concatenate(attended_t, axis=0)
    grad_v = dot(jnp.concatenate(probs_bf, axis=1), g_block[...], ((1,), (1,))).astype(BF16)

    def start_core(stage):
        core_send[stage] = total[2 * stage + 1 - core].astype(BF16)
        remote(core_send.at[stage], core_recv.at[stage], CORE_SEM + stage, sibling).start()

    def start_plane(stage):
        wait_received(core_recv.at[stage], CORE_SEM + stage)
        summed = total[2 * stage + core] + core_recv[stage].astype(F32)
        mine[stage] = summed
        plane_send[stage] = summed.astype(BF16)
        for k, (other, device) in enumerate(peers):
            remote(
                plane_send.at[stage, pl.ds(pl.multiple_of(other * 16, 16), 16)],
                plane_recv.at[stage, k],
                PLANE_SEM + stage,
                device,
            ).start()

    def start_line(stage):
        fifteen = plane_recv.at[stage]
        wait_received(fifteen, PLANE_SEM + stage)
        summed = mine[stage, pl.ds(pl.multiple_of(chip * 16, 16), 16), :]
        for k in range(NP - 1):
            summed = summed + plane_recv[stage, k].astype(F32)

        @pl.when(z != 0)
        def _():
            line_send[stage] = summed.astype(BF16)
            remote(
                line_send.at[stage], line_recv.at[stage, z], LINE_SEM + stage, z_id(0)
            ).start()

        @pl.when(z == 0)
        def _():
            mine[stage, pl.ds(0, 16), :] = summed

    here = pl.ds(pl.multiple_of(chip * 16, 16), 16)

    def spot(stage):
        return gathered.at[2 * stage + core, here]

    def start_gather(stage):
        @pl.when(z == 0)
        def _():
            wait_received(line_recv.at[stage, pl.ds(1, NZ - 1)], LINE_SEM + stage)
            summed = mine[stage, pl.ds(0, 16), :]
            for k in range(1, NZ):
                summed = summed + line_recv[stage, k].astype(F32)
            gathered[2 * stage + core, here, :] = (summed * factor).astype(BF16)

        @pl.when(z != 0)
        def _():
            wait_received(spot(stage), CAST_SEM + stage)

        @pl.when(z == 0)
        def _():
            for k in CAST_ORDER[:4]:
                remote(spot(stage), spot(stage), CAST_SEM + stage, z_id(k)).start()

        for other, device in peers:
            remote(spot(stage), spot(stage), GATHER_SEM + stage, device).start()

        @pl.when(z == 0)
        def _():
            for k in CAST_ORDER[4:]:
                remote(spot(stage), spot(stage), CAST_SEM + stage, z_id(k)).start()

    def finish_gather(stage):
        own = gathered.at[2 * stage + core]
        wait_received(own.at[pl.ds(0, 240)], GATHER_SEM + stage)
        remote(own, own, BOTH_SEM + stage, sibling).start()

    mixed_t = attended_t.astype(BF16)
    total[0] = dot(normed_t, grad_v)
    total[1] = dot(mixed_t, cot)
    start_core(0)

    grad_probs = dot(values, g_block[...])
    keys_t = keys_float.T.astype(BF16)
    grad_logits = []
    k_along = []
    grad_q_t = []
    scale_sum = jnp.zeros((1, OWN), F32)
    lane = lax.broadcasted_iota(jnp.int32, (1, OWN), 1)
    for h in range(HEADS):
        ch = slice(h * HEAD_DIM, (h + 1) * HEAD_DIM)
        ln = slice(h * OWN, (h + 1) * OWN)
        scale = scale_ref[h]
        prob = probs[h]
        grad_prob = grad_probs[:, ln]
        row_dot = jnp.sum(prob * grad_prob, axis=0, keepdims=True)
        grad_logit = prob * (grad_prob - row_dot)
        product = grad_logit * logits[h]
        along_q = jnp.sum(product, axis=0, keepdims=True)
        scale_sum = scale_sum + jnp.where(
            lane == h, jnp.sum(along_q, axis=1, keepdims=True) / scale, 0.0
        )
        k_along.append(jnp.sum(product, axis=1, keepdims=True))
        grad_logits.append((grad_logit * (q_inverse[h] * scale)).astype(BF16))
        unit_grad = dot(keys_t[ch], (grad_logit * (k_inverse[h] * scale)).astype(BF16))
        grad_q_t.append(
            q_inverse[h] * (unit_grad - query_t[ch] * (q_inverse[h] * along_q))
        )

    grad_q = jnp.concatenate(grad_q_t, axis=0).T.astype(BF16)
    grad_k_unit = dot(jnp.concatenate(grad_logits, axis=1), q_block[...], ((1,), (1,)))
    low = lax.broadcasted_iota(jnp.int32, (1, OWN), 1) < HEAD_DIM
    grad_k = []
    for t in range(2):
        ln = slice(t * OWN, (t + 1) * OWN)
        inv = jnp.where(low, k_inverse[2 * t], k_inverse[2 * t + 1])
        along = jnp.where(low, k_along[2 * t], k_along[2 * t + 1])
        grad_k.append(inv * (grad_k_unit[:, ln] - keys_float[:, ln] * (inv * along)))
    grad_k = jnp.concatenate(grad_k, axis=1).astype(BF16)

    total[2] = dot(own_normed_t, grad_q)
    total[3] = dot(normed_t, grad_k)
    start_core(1)
    start_plane(0)

    grad_kv = jnp.concatenate([grad_k, grad_v], axis=1)
    grad_normed = dot(grad_kv, w_kv, ((1,), (1,)))
    grad_normed_own = grad_normed[:OWN] + dot(grad_q, w_q, ((1,), (1,)))

    def norm_back(values, inverse, grad):
        scaled = values * inverse
        gain_term = jnp.sum(grad * scaled, axis=0, keepdims=True)
        grad = grad * gain
        along = jnp.mean(grad * scaled, axis=-1, keepdims=True)
        return gain_term, inverse * (grad - scaled * along)

    start_plane(1)

    gain_own, image_own = norm_back(own_float, own_inverse, grad_normed_own)
    gain_halo, image_halo = norm_back(halo_float, halo_inverse, grad_normed[OWN:])
    gain_sum = gain_own + gain_halo
    grad_send[...] = image_halo.astype(BF16)
    for place, step in reversed(tuple(zip(PLACES, OWNERS))):
        there = pl.ds(place[0], place[1])
        remote(grad_send.at[there], grad_back.at[there], BACK_SEM, neighbour(step)).start()
    small_own[...] = jnp.concatenate(
        [scale_sum, gain_sum[:, :OWN], gain_sum[:, OWN:], jnp.zeros((5, OWN), F32)], axis=0
    )
    remote(small_own, small_core, SMALL_CORE, sibling).start()

    start_line(0)

    wait_received(small_core, SMALL_CORE)
    chip_small = small_own[...] + small_core[...]
    small_plane[chip] = chip_small

    @pl.when(chip != 0)
    def _():
        remote(
            small_plane.at[chip], small_plane.at[chip], SMALL_PLANE, (z * 2, core)
        ).start()

    mixed = attended_t.T.astype(BF16)
    output_ref[...] = (own_float + dot(mixed, w_out_ref[...])).astype(BF16)
    store(output_ref, output_hbm)

    start_line(1)

    @pl.when(chip == 0)
    def _():
        wait_received(small_plane.at[pl.ds(1, NP - 1)], SMALL_PLANE)
        plane = small_plane[0]
        for k in range(1, NP):
            plane = plane + small_plane[k]
        small_line[z] = plane

        @pl.when(z != 0)
        def _():
            remote(small_line.at[z], small_line.at[z], SMALL_LINE, z_id(0)).start()

    wait_received(grad_back, BACK_SEM)
    grad_image = cot.astype(F32) + image_own
    grad_image = grad_image + dot(sel, grad_back[pl.ds(96, 128), :], ((0,), (0,)))
    top = grad_back[pl.ds(48, 48), :].astype(F32)
    bottom = grad_back[pl.ds(0, 48), :].astype(F32)
    grad_image = jnp.concatenate(
        [grad_image[:48] + top, grad_image[48:80], grad_image[80:] + bottom], axis=0
    )
    grad_image_ref[...] = grad_image.astype(BF16)
    store(grad_image_ref, grad_image_hbm)

    start_gather(0)
    start_gather(1)

    @pl.when(chip == 0)
    def _():
        @pl.when(z == 0)
        def _():
            wait_received(small_line.at[pl.ds(1, NZ - 1)], SMALL_LINE)
            line = small_line[0]
            for k in range(1, NZ):
                line = line + small_line[k]
            small_total[...] = line * factor

        @pl.when(z != 0)
        def _():
            wait_received(small_total, SMALL_CAST)

        for other, device in peers:
            remote(small_total, small_total, SMALL_GATHER, device).start()

        @pl.when(z == 0)
        def _():
            for k in CAST_ORDER:
                remote(small_total, small_total, SMALL_CAST, z_id(k)).start()

    finish_gather(0)
    finish_gather(1)

    @pl.when(chip != 0)
    def _():
        wait_received(small_total, SMALL_GATHER)

    store(small_total, small_hbm)

    wait_received(gathered.at[1 - core], BOTH_SEM)
    grad_out_ref[...] = gathered[1].astype(F32)
    store(grad_out_ref, grad_out_hbm)
    grad_qkv_ref[:, pl.ds(2 * C, C)] = gathered[0].astype(F32)
    value_part = pl.ds(2 * C, C)
    store(grad_qkv_ref.at[:, value_part], grad_qkv_hbm.at[:, value_part])
    wait_received(gathered.at[3 - core], BOTH_SEM + 1)
    for j in range(2):
        part = pl.ds(j * C, C)
        grad_qkv_ref[:, part] = gathered[2 + j].astype(F32)
        store(grad_qkv_ref.at[:, part], grad_qkv_hbm.at[:, part])

    wait_sent(halo, HALO_SEM)
    wait_sent(grad_send, BACK_SEM)
    wait_sent(small_own, SMALL_CORE)
    for stage in range(2):
        wait_sent(core_send.at[stage], CORE_SEM + stage)
        wait_sent(plane_recv.at[stage], PLANE_SEM + stage)
        wait_sent(gathered.at[0, pl.ds(0, 240)], GATHER_SEM + stage)
        wait_sent(gathered.at[0], BOTH_SEM + stage)

    @pl.when(z != 0)
    def _():
        for stage in range(2):
            wait_sent(line_send.at[stage], LINE_SEM + stage)

    @pl.when(z == 0)
    def _():
        for stage in range(2):
            wait_sent(line_recv.at[stage, pl.ds(1, NZ - 1)], CAST_SEM + stage)

    @pl.when(chip != 0)
    def _():
        wait_sent(small_total, SMALL_PLANE)

    @pl.when(chip == 0)
    def _():
        wait_sent(small_plane.at[pl.ds(1, NP - 1)], SMALL_GATHER)

        @pl.when(z != 0)
        def _():
            wait_sent(small_total, SMALL_LINE)

        @pl.when(z == 0)
        def _():
            wait_sent(small_line.at[pl.ds(1, NZ - 1)], SMALL_CAST)

    for copy in stores:
        copy.wait()


def deliver(
    output,
    grad_image,
    grad_qkv,
    grad_out,
    small_ref,
    output_out,
    grad_image_out,
    grad_qkv_out,
    grad_out_out,
    gain_ref,
    scale_ref,
    qkv_ref,
    out_ref,
    output_ref,
    image_ref,
    sems,
):
    steps = (
        (grad_qkv, grad_qkv_out, qkv_ref),
        (grad_out, grad_out_out, out_ref),
        (output, output_out, output_ref),
        (grad_image, grad_image_out, image_ref),
    )
    loads = [pltpu.make_async_copy(a, c, sems.at[i]) for i, (a, b, c) in enumerate(steps)]
    copies = [pltpu.make_async_copy(c, b, sems.at[4 + i]) for i, (a, b, c) in enumerate(steps)]
    for load in loads:
        load.start()
    for load, copy in zip(loads, copies):
        load.wait()
        copy.start()
    gain_ref[:, pl.ds(0, OWN)] = small_ref[pl.ds(1, 1), :]
    gain_ref[:, pl.ds(OWN, OWN)] = small_ref[pl.ds(2, 1), :]
    scale_ref[...] = small_ref[pl.ds(0, 1), pl.ds(0, HEADS)]
    for copy in copies:
        copy.wait()


def on_device(image, w_qkv, w_out, norm_gain, head_scale, cotangent):
    rows = lax.axis_size("row")
    cols = lax.axis_size("col")
    vmem = pl.BlockSpec(memory_space=pltpu.VMEM)
    hbm = pl.BlockSpec(memory_space=pl.ANY)
    smem = pl.BlockSpec(memory_space=pltpu.SMEM)
    factor = 1.0 / math.sqrt(rows * TH * cols * TW)

    def kernel(*refs):
        block(rows, cols, factor, *refs)

    parts = pl.pallas_call(
        kernel,
        out_shape=(
            jax.ShapeDtypeStruct((OWN, C), BF16),
            jax.ShapeDtypeStruct((OWN, C), BF16),
            jax.ShapeDtypeStruct((C, 3 * C), F32),
            jax.ShapeDtypeStruct((C, C), F32),
            jax.ShapeDtypeStruct((8, OWN), F32),
        ),
        in_specs=[hbm, hbm, hbm, hbm, smem, hbm],
        out_specs=(hbm,) * 5,
        scratch_shapes=[
            pltpu.VMEM((OWN, C), BF16),
            pltpu.VMEM((C, 3 * C), BF16),
            pltpu.VMEM((C, C), BF16),
            pltpu.VMEM((1, C), F32),
            pltpu.VMEM((OWN, C), BF16),
            pltpu.VMEM((HALO, C), BF16),
            pltpu.VMEM((OWN, C), BF16),
            pltpu.VMEM((HALO, C), BF16),
            pltpu.VMEM((HALO, C), BF16),
            pltpu.VMEM((C, LANES), BF16),
            pltpu.VMEM((C, LANES), BF16),
            pltpu.VMEM((4, C, C), F32),
            pltpu.VMEM((2, C, C), BF16),
            pltpu.VMEM((2, C, C), BF16),
            pltpu.VMEM((2, C, C), F32),
            pltpu.VMEM((2, C, C), BF16),
            pltpu.VMEM((2, NP - 1, 16, C), BF16),
            pltpu.VMEM((2, 16, C), BF16),
            pltpu.VMEM((2, NZ, 16, C), BF16),
            pltpu.VMEM((4, C, C), BF16),
            pltpu.VMEM((8, OWN), F32),
            pltpu.VMEM((8, OWN), F32),
            pltpu.VMEM((NP, 8, OWN), F32),
            pltpu.VMEM((NZ, 8, OWN), F32),
            pltpu.VMEM((8, OWN), F32),
            pltpu.VMEM((OWN, C), BF16),
            pltpu.VMEM((OWN, C), BF16),
            pltpu.VMEM((C, 3 * C), F32),
            pltpu.VMEM((C, C), F32),
            pltpu.SemaphoreType.DMA((38,)),
            pltpu.SemaphoreType.DMA((12,)),
        ],
        compiler_params=pltpu.CompilerParams(
            collective_id=0, has_side_effects=True, vmem_limit_bytes=VMEM_LIMIT
        ),
    )(
        image.reshape(OWN, C),
        w_qkv,
        w_out,
        norm_gain.reshape(1, C),
        head_scale,
        cotangent.reshape(OWN, C),
    )
    output, grad_image, grad_qkv, grad_out, grad_gain, grad_scale = pl.pallas_call(
        deliver,
        out_shape=(
            jax.ShapeDtypeStruct((OWN, C), BF16),
            jax.ShapeDtypeStruct((OWN, C), BF16),
            jax.ShapeDtypeStruct((C, 3 * C), F32),
            jax.ShapeDtypeStruct((C, C), F32),
            jax.ShapeDtypeStruct((1, C), F32),
            jax.ShapeDtypeStruct((1, HEADS), F32),
        ),
        in_specs=[hbm, hbm, hbm, hbm, vmem],
        out_specs=(hbm, hbm, hbm, hbm, vmem, vmem),
        scratch_shapes=[
            pltpu.VMEM((C, 3 * C), F32),
            pltpu.VMEM((C, C), F32),
            pltpu.VMEM((OWN, C), BF16),
            pltpu.VMEM((OWN, C), BF16),
            pltpu.SemaphoreType.DMA((8,)),
        ],
        compiler_params=pltpu.CompilerParams(vmem_limit_bytes=VMEM_LIMIT),
    )(*parts)
    return (
        output.reshape(TH, TW, C),
        grad_image.reshape(TH, TW, C),
        grad_qkv,
        grad_out,
        grad_gain.reshape(C),
        grad_scale.reshape(HEADS),
    )


def solution(mesh):
    placed = (P("row", "col", None), P(), P(), P(), P(), P("row", "col", None))
    return jax.shard_map(
        on_device,
        mesh=mesh,
        in_specs=placed,
        out_specs=(P("row", "col", None), P("row", "col", None), P(), P(), P(), P()),
        check_vma=False,
    )
```

time: 67.1 us -> 50.3 us (0.75)
  the two profiles are of different devices: /device:TPU:1 before, /device:TPU:33 now
where the time goes in v2:
time: 50.3 us; the launch traced here: 50.1 us
  Pallas kernels  49.5 us (98%)
  between operations  0.64 us (1%)
    pallas_call x1, Pallas kernels, on_device(): pl.pallas_call(kernel, out_shape=(jax.ShapeDtypeStruct((OWN, C), BF16), j...  46.1 us
    pallas_call x1, Pallas kernels, on_device(): pl.pallas_call(deliver, out_shape=(jax.ShapeDtypeStruct((OWN, C), BF16),...  3.43 us

profile of v2, /device:TPU:33, one launch (start us, length us, event | category | flops | bytes accessed | tf_op | source)
XLA Modules:
  0.0 50.1 jit_solution(11773275727739307720)
XLA Ops:
  0.6 46.1 %shard_map.109 = (bf16[128,256]{1,0:T(8,128)(2,1)}, bf16[128,256]{1,0:T(8,128)(2,1)}, f32[256,768]{1,0:T(8,128)}, f32[256,256]{1,0:T(8,128)}, f32[8,128]{1,0:T(8,128)}) custom-call(bf16[128,256]{1,0:T(8,128)(2,1)} %bitcast.7, bf16[256,768]{1,0:T(8,128)(2,1)} %refs_1_.1, bf16[256,256]{1,0:T(8,128)(2,1)} %refs_2_.1, f32[1,256]{1,0:T(1,128)} %bitcast.9, ...), custom_call_target="tpu_custom_call" | custom-call | tf_op jit(solution)/shard_map/pallas_call | solution.py:618
  46.7 3.4 %shard_map.110 = (bf16[128,256]{1,0:T(8,128)(2,1)}, bf16[128,256]{1,0:T(8,128)(2,1)}, f32[256,768]{1,0:T(8,128)}, f32[256,256]{1,0:T(8,128)}, f32[1,256]{1,0:T(1,128)}, /*index=5*/f32[1,4]{1,0:T(1,128)}) custom-call(bf16[128,256]{1,0:T(8,128)(2,1)} %get-tuple-element.17.output, bf16[128,256]{1,0:T(8,128)(2,1)} %get-tuple-element.18.grad_image, ...), custom_call_target="tpu_custom_call" | custom-call | tf_op jit(solution)/shard_map/pallas_call | solution.py:673

commit v3 on v2

--- a/solution.py
+++ b/solution.py
@@ -19,7 +19,7 @@
 LANES = HEADS * OWN
 EPS = 1e-06
 NP = 16
-VMEM_LIMIT = 60 * 1024 * 1024
+VMEM_LIMIT = 40 * 1024 * 1024
 NZ = 16
 MESH = pl.DeviceIdType.MESH
 F32 = jnp.float32
@@ -89,17 +89,18 @@
         w_qkv_hbm,
         w_out_hbm,
         gain_hbm,
-        scale_ref,
+        scale_hbm,
         cot_hbm,
-        output_hbm,
-        grad_image_hbm,
-        grad_qkv_hbm,
-        grad_out_hbm,
-        small_hbm,
+        output_ref,
+        grad_image_ref,
+        grad_qkv_ref,
+        grad_out_ref,
+        small_total,
         image_ref,
         w_qkv_ref,
         w_out_ref,
         gain_ref,
+        scale_ref,
         cot_ref,
         halo,
         side,
@@ -120,11 +121,6 @@
         small_core,
         small_plane,
         small_line,
-        small_total,
-        output_ref,
-        grad_image_ref,
-        grad_qkv_ref,
-        grad_out_ref,
         sems,
         local_sems,
     ) = refs
@@ -145,18 +141,12 @@
             (cot_hbm, cot_ref),
             (w_out_hbm, w_out_ref),
             (gain_hbm, gain_ref),
+            (scale_hbm, scale_ref),
         )
     ):
         load = pltpu.make_async_copy(src, dst, local_sems.at[i])
         load.start()
         loads.append(load)
-
-    stores = []
-
-    def store(src, dst):
-        copy = pltpu.make_async_copy(src, dst, local_sems.at[len(loads) + len(stores)])
-        copy.start()
-        stores.append(copy)
 
     def chip_id(ox, oy):
         return (z * 2 + ox % 2, (ox // 2) * 8 + oy * 2 + core)
@@ -285,7 +275,7 @@
         ln = slice(h * OWN, (h + 1) * OWN)
         k_part = keys_float[:, ch]
         k_inv = lax.rsqrt(jnp.sum(k_part * k_part, axis=1, keepdims=True) + EPS)
-        logit = scores[:, ln] * k_inv * (q_inverse[h] * scale_ref[h])
+        logit = scores[:, ln] * k_inv * (q_inverse[h] * scale_ref[0, h])
         weight = jnp.exp(logit) * mask
         prob = weight * (1.0 / jnp.sum(weight, axis=0, keepdims=True))
         probs.append(prob)
@@ -382,7 +372,7 @@
     for h in range(HEADS):
         ch = slice(h * HEAD_DIM, (h + 1) * HEAD_DIM)
         ln = slice(h * OWN, (h + 1) * OWN)
-        scale = scale_ref[h]
+        scale = scale_ref[0, h]
         prob = probs[h]
         grad_prob = grad_probs[:, ln]
         row_dot = jnp.sum(prob * grad_prob, axis=0, keepdims=True)
@@ -454,7 +444,6 @@
 
     mixed = attended_t.T.astype(BF16)
     output_ref[...] = (own_float + dot(mixed, w_out_ref[...])).astype(BF16)
-    store(output_ref, output_hbm)
 
     start_line(1)
 
@@ -479,7 +468,6 @@
         [grad_image[:48] + top, grad_image[48:80], grad_image[80:] + bottom], axis=0
     )
     grad_image_ref[...] = grad_image.astype(BF16)
-    store(grad_image_ref, grad_image_hbm)
 
     start_gather(0)
     start_gather(1)
@@ -513,19 +501,14 @@
     def _():
         wait_received(small_total, SMALL_GATHER)
 
-    store(small_total, small_hbm)
 
     wait_received(gathered.at[1 - core], BOTH_SEM)
     grad_out_ref[...] = gathered[1].astype(F32)
-    store(grad_out_ref, grad_out_hbm)
     grad_qkv_ref[:, pl.ds(2 * C, C)] = gathered[0].astype(F32)
-    value_part = pl.ds(2 * C, C)
-    store(grad_qkv_ref.at[:, value_part], grad_qkv_hbm.at[:, value_part])
     wait_received(gathered.at[3 - core], BOTH_SEM + 1)
     for j in range(2):
         part = pl.ds(j * C, C)
         grad_qkv_ref[:, part] = gathered[2 + j].astype(F32)
-        store(grad_qkv_ref.at[:, part], grad_qkv_hbm.at[:, part])
 
     wait_sent(halo, HALO_SEM)
     wait_sent(grad_send, BACK_SEM)
@@ -562,44 +545,39 @@
         def _():
             wait_sent(small_line.at[pl.ds(1, NZ - 1)], SMALL_CAST)
 
-    for copy in stores:
-        copy.wait()
-
 
 def deliver(
     output,
     grad_image,
     grad_qkv,
     grad_out,
-    small_ref,
+    small,
     output_out,
     grad_image_out,
     grad_qkv_out,
     grad_out_out,
+    gain_out,
+    scale_out,
     gain_ref,
     scale_ref,
-    qkv_ref,
-    out_ref,
-    output_ref,
-    image_ref,
     sems,
 ):
     steps = (
-        (grad_qkv, grad_qkv_out, qkv_ref),
-        (grad_out, grad_out_out, out_ref),
-        (output, output_out, output_ref),
-        (grad_image, grad_image_out, image_ref),
+        (grad_qkv, grad_qkv_out),
+        (grad_out, grad_out_out),
+        (output, output_out),
+        (grad_image, grad_image_out),
+        (gain_ref, gain_out),
+        (scale_ref, scale_out),
     )
-    loads = [pltpu.make_async_copy(a, c, sems.at[i]) for i, (a, b, c) in enumerate(steps)]
-    copies = [pltpu.make_async_copy(c, b, sems.at[4 + i]) for i, (a, b, c) in enumerate(steps)]
-    for load in loads:
-        load.start()
-    for load, copy in zip(loads, copies):
-        load.wait()
+    copies = [pltpu.make_async_copy(a, b, sems.at[i]) for i, (a, b) in enumerate(steps)]
+    for copy in copies[:4]:
         copy.start()
-    gain_ref[:, pl.ds(0, OWN)] = small_ref[pl.ds(1, 1), :]
-    gain_ref[:, pl.ds(OWN, OWN)] = small_ref[pl.ds(2, 1), :]
-    scale_ref[...] = small_ref[pl.ds(0, 1), pl.ds(0, HEADS)]
+    gain_ref[:, pl.ds(0, OWN)] = small[pl.ds(1, 1), :]
+    gain_ref[:, pl.ds(OWN, OWN)] = small[pl.ds(2, 1), :]
+    scale_ref[...] = small[pl.ds(0, 1), pl.ds(0, HEADS)]
+    for copy in copies[4:]:
+        copy.start()
     for copy in copies:
         copy.wait()
 
@@ -609,28 +587,31 @@
     cols = lax.axis_size("col")
     vmem = pl.BlockSpec(memory_space=pltpu.VMEM)
     hbm = pl.BlockSpec(memory_space=pl.ANY)
-    smem = pl.BlockSpec(memory_space=pltpu.SMEM)
     factor = 1.0 / math.sqrt(rows * TH * cols * TW)
 
     def kernel(*refs):
         block(rows, cols, factor, *refs)
+
+    def pinned(array):
+        return pltpu.with_memory_space_constraint(array, pltpu.HBM)
 
     parts = pl.pallas_call(
         kernel,
         out_shape=(
-            jax.ShapeDtypeStruct((OWN, C), BF16),
-            jax.ShapeDtypeStruct((OWN, C), BF16),
-            jax.ShapeDtypeStruct((C, 3 * C), F32),
-            jax.ShapeDtypeStruct((C, C), F32),
-            jax.ShapeDtypeStruct((8, OWN), F32),
+            pltpu.VMEM((OWN, C), BF16),
+            pltpu.VMEM((OWN, C), BF16),
+            pltpu.VMEM((C, 3 * C), F32),
+            pltpu.VMEM((C, C), F32),
+            pltpu.VMEM((8, OWN), F32),
         ),
-        in_specs=[hbm, hbm, hbm, hbm, smem, hbm],
-        out_specs=(hbm,) * 5,
+        in_specs=[hbm] * 6,
+        out_specs=(vmem,) * 5,
         scratch_shapes=[
             pltpu.VMEM((OWN, C), BF16),
             pltpu.VMEM((C, 3 * C), BF16),
             pltpu.VMEM((C, C), BF16),
             pltpu.VMEM((1, C), F32),
+            pltpu.SMEM((1, HEADS), F32),
             pltpu.VMEM((OWN, C), BF16),
             pltpu.VMEM((HALO, C), BF16),
             pltpu.VMEM((OWN, C), BF16),
@@ -651,24 +632,24 @@
             pltpu.VMEM((8, OWN), F32),
             pltpu.VMEM((NP, 8, OWN), F32),
             pltpu.VMEM((NZ, 8, OWN), F32),
-            pltpu.VMEM((8, OWN), F32),
-            pltpu.VMEM((OWN, C), BF16),
-            pltpu.VMEM((OWN, C), BF16),
-            pltpu.VMEM((C, 3 * C), F32),
-            pltpu.VMEM((C, C), F32),
             pltpu.SemaphoreType.DMA((38,)),
-            pltpu.SemaphoreType.DMA((12,)),
+            pltpu.SemaphoreType.DMA((6,)),
         ],
         compiler_params=pltpu.CompilerParams(
             collective_id=0, has_side_effects=True, vmem_limit_bytes=VMEM_LIMIT
         ),
     )(
-        image.reshape(OWN, C),
-        w_qkv,
-        w_out,
-        norm_gain.reshape(1, C),
-        head_scale,
-        cotangent.reshape(OWN, C),
+        *map(
+            pinned,
+            (
+                image.reshape(OWN, C),
+                w_qkv,
+                w_out,
+                norm_gain.reshape(1, C),
+                head_scale.reshape(1, HEADS),
+                cotangent.reshape(OWN, C),
+            ),
+        )
     )
     output, grad_image, grad_qkv, grad_out, grad_gain, grad_scale = pl.pallas_call(
         deliver,
@@ -680,17 +661,15 @@
             jax.ShapeDtypeStruct((1, C), F32),
             jax.ShapeDtypeStruct((1, HEADS), F32),
         ),
-        in_specs=[hbm, hbm, hbm, hbm, vmem],
-        out_specs=(hbm, hbm, hbm, hbm, vmem, vmem),
+        in_specs=[vmem] * 5,
+        out_specs=(hbm,) * 6,
         scratch_shapes=[
-            pltpu.VMEM((C, 3 * C), F32),
-            pltpu.VMEM((C, C), F32),
-            pltpu.VMEM((OWN, C), BF16),
-            pltpu.VMEM((OWN, C), BF16),
-            pltpu.SemaphoreType.DMA((8,)),
+            pltpu.VMEM((1, C), F32),
+            pltpu.VMEM((1, HEADS), F32),
+            pltpu.SemaphoreType.DMA((6,)),
         ],
         compiler_params=pltpu.CompilerParams(vmem_limit_bytes=VMEM_LIMIT),
-    )(*parts)
+    )(*(pltpu.with_memory_space_constraint(part, pltpu.VMEM) for part in parts))
     return (
         output.reshape(TH, TW, C),
         grad_image.reshape(TH, TW, C),

time: 50.3 us -> 46.4 us (0.922)
  Pallas kernels: 49.5 us -> 45.6 us
    pallas_call x1, Pallas kernels: 3.43 us -> 1.06 us  [on_device(): pl.pallas_call(deliver, out_shape=(jax.ShapeDtypeStruct((OWN, C), BF16),...]
    pallas_call x1, Pallas kernels: 46.1 us -> 44.6 us  [on_device(): pl.pallas_call(kernel, out_shape=(pltpu.VMEM((OWN, C), BF16), pltpu.VMEM(...]
where the time goes in v3:
time: 46.4 us; the launch traced here: 46.3 us
  Pallas kernels  45.6 us (98%)
  between operations  0.64 us (1%)
    pallas_call x1, Pallas kernels, on_device(): pl.pallas_call(kernel, out_shape=(pltpu.VMEM((OWN, C), BF16), pltpu.VMEM(...  44.6 us
    pallas_call x1, Pallas kernels, on_device(): pl.pallas_call(deliver, out_shape=(jax.ShapeDtypeStruct((OWN, C), BF16),...  1.06 us

profile of v3, /device:TPU:33, one launch (start us, length us, event | category | flops | bytes accessed | tf_op | source)
XLA Modules:
  0.0 46.3 jit_solution(16774651221188817565)
XLA Ops:
  0.6 44.6 %shard_map.109 = (bf16[128,256]{1,0:T(8,128)(2,1)S(1)}, bf16[128,256]{1,0:T(8,128)(2,1)S(1)}, f32[256,768]{1,0:T(8,128)S(1)}, f32[256,256]{1,0:T(8,128)S(1)}, f32[8,128]{1,0:T(8,128)S(1)}) custom-call(bf16[128,256]{1,0:T(8,128)(2,1)} %bitcast.8, bf16[256,768]{1,0:T(8,128)(2,1)} %refs_1_.1, bf16[256,256]{1,0:T(8,128)(2,1)} %refs_2_.1, f32[1,256]{1,0:T(1,128)} %bitcast.10, ...), custom_call_target="tpu_custom_call" | custom-call | tf_op jit(solution)/shard_map/pallas_call | solution.py:598
  45.2 1.1 %shard_map.110 = (bf16[128,256]{1,0:T(8,128)(2,1)}, bf16[128,256]{1,0:T(8,128)(2,1)}, f32[256,768]{1,0:T(8,128)}, f32[256,256]{1,0:T(8,128)}, f32[1,256]{1,0:T(1,128)}, /*index=5*/f32[1,4]{1,0:T(1,128)}) custom-call(bf16[128,256]{1,0:T(8,128)(2,1)S(1)} %get-tuple-element.17.output, bf16[128,256]{1,0:T(8,128)(2,1)S(1)} %get-tuple-element.18.grad_image, ...), custom_call_target="tpu_custom_call" | custom-call | tf_op jit(solution)/shard_map/pallas_call | solution.py:654

commit v4 on v3

--- a/solution.py
+++ b/solution.py
@@ -41,9 +41,12 @@
     ((dx, dy) for dx in range(4) for dy in range(4) if dx or dy),
     key=lambda step: (-min(step[0], 4 - step[0]) - min(step[1], 4 - step[1]), step),
 )
-CAST_ORDER = (1, 2, 3, 4, 5, 15, 6, 14, 7, 13, 8, 12, 9, 11, 10)
+OWNER_PLANES = 2
+CASTS = ((10, 11, 12, 13, 14, 15), (2, 3, 4, 5, 6, 7, 8, 9))
+CASTS_FIRST = (2, 4)
 HALO_SEM, BACK_SEM, SMALL_CORE, SMALL_PLANE, SMALL_LINE, SMALL_CAST, SMALL_GATHER = range(7)
-CORE_SEM, PLANE_SEM, LINE_SEM, CAST_SEM, GATHER_SEM, BOTH_SEM = range(7, 19, 2)
+CAST_SEM, GATHER_SEM, BOTH_SEM = range(7, 10)
+CORE_SEM, PLANE_SEM, LINE_SEM = range(10, 16, 2)
 
 
 def dot(a, b, contract=((1,), (0,))):
@@ -172,14 +175,14 @@
     for other, device in peers:
         greet(device)
 
-    @pl.when(z != 0)
-    def _():
-        greet(z_id(0))
-
-    @pl.when(z == 0)
+    @pl.when(z < OWNER_PLANES)
     def _():
         for k in range(1, NZ):
-            greet(z_id(k))
+            greet(z_id(lax.rem(z + k, NZ)))
+
+    @pl.when(z >= OWNER_PLANES)
+    def _():
+        greet(z_id(jnp.where(z >= 10, 0, 1)))
 
     def remote(src, dst, sem, device):
         return pltpu.make_async_remote_copy(
@@ -201,13 +204,15 @@
     loads[0].wait()
     side[...] = dot(sel, image_ref[...]).astype(BF16)
 
-    @pl.when(z != 0)
-    def _():
-        pl.semaphore_wait(barrier, 8 + (NP - 1) + 1)
-
-    @pl.when(z == 0)
-    def _():
-        pl.semaphore_wait(barrier, 8 + (NP - 1) + (NZ - 1))
+    @pl.when(z >= OWNER_PLANES)
+    def _():
+        pl.semaphore_wait(barrier, 8 + (NP - 1) + OWNER_PLANES)
+
+    for owner in range(OWNER_PLANES):
+
+        @pl.when(z == owner)
+        def _():
+            pl.semaphore_wait(barrier, 8 + (NP - 1) + 1 + len(CASTS[owner]))
 
     for place, step in reversed(tuple(zip(PLACES, OWNERS))):
         first, count = place[0], place[1]
@@ -249,42 +254,58 @@
         q_block[ch, ln] = part.astype(BF16)
         g_block[ch, ln] = grad_mixed_t[ch].astype(BF16)
         q_inverse.append(lax.rsqrt(jnp.sum(part * part, axis=0, keepdims=True) + EPS))
-    own_kv = dot(own_normed, w_kv)
+
+    def segment(normed, mask_part):
+        kv = dot(normed, w_kv).astype(BF16)
+        keys = kv[:, :C]
+        values = kv[:, C:]
+        keys_float = keys.astype(F32)
+        scores = dot(keys, q_block[...])
+        weights = []
+        logits = []
+        inverses = []
+        for h in range(HEADS):
+            k_part = keys_float[:, h * HEAD_DIM : (h + 1) * HEAD_DIM]
+            inverse = lax.rsqrt(jnp.sum(k_part * k_part, axis=1, keepdims=True) + EPS)
+            logit = scores[:, h * OWN : (h + 1) * OWN] * inverse
+            logit = logit * (q_inverse[h] * scale_ref[0, h])
+            weights.append(jnp.exp(logit) * mask_part)
+            logits.append(logit)
+            inverses.append(inverse)
+        keys_t = keys_float.T.astype(BF16)
+        values_t = values.astype(F32).T.astype(BF16)
+        grad_probs = dot(values, g_block[...])
+        return keys_float, keys_t, values_t, weights, logits, inverses, grad_probs
+
+    own_part = segment(own_normed, mask[:OWN])
 
     wait_received(halo, HALO_SEM)
 
     halo_float = halo[...].astype(F32)
     halo_inverse, halo_normed = norm(halo_float)
     halo_normed_t = halo_normed.astype(F32).T.astype(BF16)
-    halo_kv = dot(halo_normed, w_kv)
-    kv = jnp.concatenate([own_kv, halo_kv], axis=0).astype(BF16)
-    keys = kv[:, :C]
-    values = kv[:, C:]
-    keys_float = keys.astype(F32)
-    values_t = values.astype(F32).T.astype(BF16)
-    normed_t = jnp.concatenate([own_normed_t, halo_normed_t], axis=1)
-
-    scores = dot(keys, q_block[...])
-    probs = []
-    probs_bf = []
-    logits = []
-    k_inverse = []
+    parts = (own_part, segment(halo_normed, mask[OWN:]))
+    normed_t = (own_normed_t, halo_normed_t)
+    probs = ([], [])
+    probs_bf = ([], [])
     attended_t = []
     for h in range(HEADS):
         ch = slice(h * HEAD_DIM, (h + 1) * HEAD_DIM)
-        ln = slice(h * OWN, (h + 1) * OWN)
-        k_part = keys_float[:, ch]
-        k_inv = lax.rsqrt(jnp.sum(k_part * k_part, axis=1, keepdims=True) + EPS)
-        logit = scores[:, ln] * k_inv * (q_inverse[h] * scale_ref[0, h])
-        weight = jnp.exp(logit) * mask
-        prob = weight * (1.0 / jnp.sum(weight, axis=0, keepdims=True))
-        probs.append(prob)
-        probs_bf.append(prob.astype(BF16))
-        logits.append(logit)
-        k_inverse.append(k_inv)
-        attended_t.append(dot(values_t[ch], probs_bf[h]))
+        weights = [part[3][h] for part in parts]
+        weight_sum = sum(jnp.sum(weight, axis=0, keepdims=True) for weight in weights)
+        inverse_sum = 1.0 / weight_sum
+        mixed_head = 0.0
+        for i in range(2):
+            prob = weights[i] * inverse_sum
+            probs[i].append(prob)
+            probs_bf[i].append(prob.astype(BF16))
+            mixed_head = mixed_head + dot(parts[i][2][ch], probs_bf[i][h])
+        attended_t.append(mixed_head)
     attended_t = jnp.concatenate(attended_t, axis=0)
-    grad_v = dot(jnp.concatenate(probs_bf, axis=1), g_block[...], ((1,), (1,))).astype(BF16)
+    grad_v = [
+        dot(jnp.concatenate(probs_bf[i], axis=1), g_block[...], ((1,), (1,))).astype(BF16)
+        for i in range(2)
+    ]
 
     def start_core(stage):
         core_send[stage] = total[2 * stage + 1 - core].astype(BF16)
@@ -310,62 +331,68 @@
         for k in range(NP - 1):
             summed = summed + plane_recv[stage, k].astype(F32)
 
-        @pl.when(z != 0)
-        def _():
-            line_send[stage] = summed.astype(BF16)
-            remote(
-                line_send.at[stage], line_recv.at[stage, z], LINE_SEM + stage, z_id(0)
-            ).start()
-
-        @pl.when(z == 0)
-        def _():
-            mine[stage, pl.ds(0, 16), :] = summed
-
-    here = pl.ds(pl.multiple_of(chip * 16, 16), 16)
-
-    def spot(stage):
-        return gathered.at[2 * stage + core, here]
-
-    def start_gather(stage):
-        @pl.when(z == 0)
-        def _():
-            wait_received(line_recv.at[stage, pl.ds(1, NZ - 1)], LINE_SEM + stage)
-            summed = mine[stage, pl.ds(0, 16), :]
-            for k in range(1, NZ):
-                summed = summed + line_recv[stage, k].astype(F32)
-            gathered[2 * stage + core, here, :] = (summed * factor).astype(BF16)
-
-        @pl.when(z != 0)
-        def _():
-            wait_received(spot(stage), CAST_SEM + stage)
-
-        @pl.when(z == 0)
-        def _():
-            for k in CAST_ORDER[:4]:
-                remote(spot(stage), spot(stage), CAST_SEM + stage, z_id(k)).start()
+        summed = summed.astype(BF16)
+
+        line_send[stage] = summed
+        slot = line_recv.at[stage, z]
+
+        @pl.when(z >= OWNER_PLANES)
+        def _():
+            for k in range(OWNER_PLANES):
+                remote(line_send.at[stage], slot, LINE_SEM + stage, z_id(k)).start()
+
+        @pl.when(z < OWNER_PLANES)
+        def _():
+            line_recv[stage, z] = summed
+            remote(line_send.at[stage], slot, LINE_SEM + stage, z_id(1 - z)).start()
+
+    def cast(ref, sem, ahead):
+        for owner in range(OWNER_PLANES):
+
+            @pl.when(z == owner)
+            def _():
+                first = CASTS_FIRST[owner]
+                for k in CASTS[owner][:first] if ahead else CASTS[owner][first:]:
+                    remote(ref, ref, sem, z_id(k)).start()
+
+    spot = gathered.at[core, chip]
+    own_half = gathered.at[core]
+
+    def start_gather():
+        @pl.when(z < OWNER_PLANES)
+        def _():
+            for stage in range(2):
+                wait_received(line_recv.at[stage, pl.ds(0, NZ - 1)], LINE_SEM + stage)
+                summed = line_recv[stage, 0].astype(F32)
+                for k in range(1, NZ):
+                    summed = summed + line_recv[stage, k].astype(F32)
+                gathered[core, chip, stage] = (summed * factor).astype(BF16)
+
+        cast(spot, CAST_SEM, True)
+
+        @pl.when(z >= OWNER_PLANES)
+        def _():
+            wait_received(spot, CAST_SEM)
 
         for other, device in peers:
-            remote(spot(stage), spot(stage), GATHER_SEM + stage, device).start()
-
-        @pl.when(z == 0)
-        def _():
-            for k in CAST_ORDER[4:]:
-                remote(spot(stage), spot(stage), CAST_SEM + stage, z_id(k)).start()
-
-    def finish_gather(stage):
-        own = gathered.at[2 * stage + core]
-        wait_received(own.at[pl.ds(0, 240)], GATHER_SEM + stage)
-        remote(own, own, BOTH_SEM + stage, sibling).start()
+            remote(spot, spot, GATHER_SEM, device).start()
+
+    def deliver_half(side):
+        values = [gathered[side, :, stage].reshape(C, C).astype(F32) for stage in range(2)]
+        if side == 0:
+            grad_qkv_ref[:, pl.ds(2 * C, C)] = values[0]
+            grad_qkv_ref[:, pl.ds(0, C)] = values[1]
+        else:
+            grad_out_ref[...] = values[0]
+            grad_qkv_ref[:, pl.ds(C, C)] = values[1]
 
     mixed_t = attended_t.astype(BF16)
-    total[0] = dot(normed_t, grad_v)
+    total[0] = dot(normed_t[0], grad_v[0]) + dot(normed_t[1], grad_v[1])
     total[1] = dot(mixed_t, cot)
     start_core(0)
 
-    grad_probs = dot(values, g_block[...])
-    keys_t = keys_float.T.astype(BF16)
-    grad_logits = []
-    k_along = []
+    grad_logits = ([], [])
+    k_along = ([], [])
     grad_q_t = []
     scale_sum = jnp.zeros((1, OWN), F32)
     lane = lax.broadcasted_iota(jnp.int32, (1, OWN), 1)
@@ -373,41 +400,52 @@
         ch = slice(h * HEAD_DIM, (h + 1) * HEAD_DIM)
         ln = slice(h * OWN, (h + 1) * OWN)
         scale = scale_ref[0, h]
-        prob = probs[h]
-        grad_prob = grad_probs[:, ln]
-        row_dot = jnp.sum(prob * grad_prob, axis=0, keepdims=True)
-        grad_logit = prob * (grad_prob - row_dot)
-        product = grad_logit * logits[h]
-        along_q = jnp.sum(product, axis=0, keepdims=True)
+        grad_probs = [part[6][:, ln] for part in parts]
+        row_dot = sum(
+            jnp.sum(probs[i][h] * grad_probs[i], axis=0, keepdims=True) for i in range(2)
+        )
+        along_q = 0.0
+        unit_grad = 0.0
+        for i in range(2):
+            grad_logit = probs[i][h] * (grad_probs[i] - row_dot)
+            product = grad_logit * parts[i][4][h]
+            along_q = along_q + jnp.sum(product, axis=0, keepdims=True)
+            k_along[i].append(jnp.sum(product, axis=1, keepdims=True))
+            grad_logits[i].append((grad_logit * (q_inverse[h] * scale)).astype(BF16))
+            unit_grad = unit_grad + dot(
+                parts[i][1][ch], (grad_logit * (parts[i][5][h] * scale)).astype(BF16)
+            )
         scale_sum = scale_sum + jnp.where(
             lane == h, jnp.sum(along_q, axis=1, keepdims=True) / scale, 0.0
         )
-        k_along.append(jnp.sum(product, axis=1, keepdims=True))
-        grad_logits.append((grad_logit * (q_inverse[h] * scale)).astype(BF16))
-        unit_grad = dot(keys_t[ch], (grad_logit * (k_inverse[h] * scale)).astype(BF16))
         grad_q_t.append(
             q_inverse[h] * (unit_grad - query_t[ch] * (q_inverse[h] * along_q))
         )
 
+    start_plane(0)
     grad_q = jnp.concatenate(grad_q_t, axis=0).T.astype(BF16)
-    grad_k_unit = dot(jnp.concatenate(grad_logits, axis=1), q_block[...], ((1,), (1,)))
     low = lax.broadcasted_iota(jnp.int32, (1, OWN), 1) < HEAD_DIM
     grad_k = []
-    for t in range(2):
-        ln = slice(t * OWN, (t + 1) * OWN)
-        inv = jnp.where(low, k_inverse[2 * t], k_inverse[2 * t + 1])
-        along = jnp.where(low, k_along[2 * t], k_along[2 * t + 1])
-        grad_k.append(inv * (grad_k_unit[:, ln] - keys_float[:, ln] * (inv * along)))
-    grad_k = jnp.concatenate(grad_k, axis=1).astype(BF16)
+    for i in range(2):
+        unit_grad = dot(jnp.concatenate(grad_logits[i], axis=1), q_block[...], ((1,), (1,)))
+        keys_float, inverses = parts[i][0], parts[i][5]
+        pieces = []
+        for t in range(2):
+            ln = slice(t * OWN, (t + 1) * OWN)
+            inv = jnp.where(low, inverses[2 * t], inverses[2 * t + 1])
+            along = jnp.where(low, k_along[i][2 * t], k_along[i][2 * t + 1])
+            pieces.append(inv * (unit_grad[:, ln] - keys_float[:, ln] * (inv * along)))
+        grad_k.append(jnp.concatenate(pieces, axis=1).astype(BF16))
 
     total[2] = dot(own_normed_t, grad_q)
-    total[3] = dot(normed_t, grad_k)
+    total[3] = dot(normed_t[0], grad_k[0]) + dot(normed_t[1], grad_k[1])
     start_core(1)
-    start_plane(0)
-
-    grad_kv = jnp.concatenate([grad_k, grad_v], axis=1)
-    grad_normed = dot(grad_kv, w_kv, ((1,), (1,)))
-    grad_normed_own = grad_normed[:OWN] + dot(grad_q, w_q, ((1,), (1,)))
+
+    grad_normed = [
+        dot(jnp.concatenate([grad_k[i], grad_v[i]], axis=1), w_kv, ((1,), (1,)))
+        for i in range(2)
+    ]
+    grad_normed[0] = grad_normed[0] + dot(grad_q, w_q, ((1,), (1,)))
 
     def norm_back(values, inverse, grad):
         scaled = values * inverse
@@ -416,19 +454,20 @@
         along = jnp.mean(grad * scaled, axis=-1, keepdims=True)
         return gain_term, inverse * (grad - scaled * along)
 
+    gain_own, image_own = norm_back(own_float, own_inverse, grad_normed[0])
+    gain_halo, image_halo = norm_back(halo_float, halo_inverse, grad_normed[1])
+    gain_sum = gain_own + gain_halo
+    small_own[...] = jnp.concatenate(
+        [scale_sum, gain_sum[:, :OWN], gain_sum[:, OWN:], jnp.zeros((5, OWN), F32)], axis=0
+    )
+    remote(small_own, small_core, SMALL_CORE, sibling).start()
+
     start_plane(1)
 
-    gain_own, image_own = norm_back(own_float, own_inverse, grad_normed_own)
-    gain_halo, image_halo = norm_back(halo_float, halo_inverse, grad_normed[OWN:])
-    gain_sum = gain_own + gain_halo
     grad_send[...] = image_halo.astype(BF16)
     for place, step in reversed(tuple(zip(PLACES, OWNERS))):
         there = pl.ds(place[0], place[1])
         remote(grad_send.at[there], grad_back.at[there], BACK_SEM, neighbour(step)).start()
-    small_own[...] = jnp.concatenate(
-        [scale_sum, gain_sum[:, :OWN], gain_sum[:, OWN:], jnp.zeros((5, OWN), F32)], axis=0
-    )
-    remote(small_own, small_core, SMALL_CORE, sibling).start()
 
     start_line(0)
 
@@ -455,9 +494,16 @@
             plane = plane + small_plane[k]
         small_line[z] = plane
 
-        @pl.when(z != 0)
-        def _():
-            remote(small_line.at[z], small_line.at[z], SMALL_LINE, z_id(0)).start()
+        slot = small_line.at[z]
+
+        @pl.when(z >= OWNER_PLANES)
+        def _():
+            for k in range(OWNER_PLANES):
+                remote(slot, slot, SMALL_LINE, z_id(k)).start()
+
+        @pl.when(z < OWNER_PLANES)
+        def _():
+            remote(slot, slot, SMALL_LINE, z_id(1 - z)).start()
 
     wait_received(grad_back, BACK_SEM)
     grad_image = cot.astype(F32) + image_own
@@ -469,65 +515,80 @@
     )
     grad_image_ref[...] = grad_image.astype(BF16)
 
-    start_gather(0)
-    start_gather(1)
+    start_gather()
 
     @pl.when(chip == 0)
     def _():
-        @pl.when(z == 0)
-        def _():
-            wait_received(small_line.at[pl.ds(1, NZ - 1)], SMALL_LINE)
+        @pl.when(z < OWNER_PLANES)
+        def _():
+            wait_received(small_line.at[pl.ds(0, NZ - 1)], SMALL_LINE)
             line = small_line[0]
             for k in range(1, NZ):
                 line = line + small_line[k]
             small_total[...] = line * factor
 
-        @pl.when(z != 0)
+        cast(small_total, SMALL_CAST, True)
+
+        @pl.when(z >= OWNER_PLANES)
         def _():
             wait_received(small_total, SMALL_CAST)
 
         for other, device in peers:
             remote(small_total, small_total, SMALL_GATHER, device).start()
 
-        @pl.when(z == 0)
-        def _():
-            for k in CAST_ORDER:
-                remote(small_total, small_total, SMALL_CAST, z_id(k)).start()
-
-    finish_gather(0)
-    finish_gather(1)
+        cast(small_total, SMALL_CAST, False)
+
+    cast(spot, CAST_SEM, False)
+
+    wait_received(gathered.at[0, pl.ds(0, NP - 1)], GATHER_SEM)
+    remote(own_half, own_half, BOTH_SEM, sibling).start()
+
+    @pl.when(core == 0)
+    def _():
+        deliver_half(0)
+
+    @pl.when(core == 1)
+    def _():
+        deliver_half(1)
 
     @pl.when(chip != 0)
     def _():
         wait_received(small_total, SMALL_GATHER)
 
-
     wait_received(gathered.at[1 - core], BOTH_SEM)
-    grad_out_ref[...] = gathered[1].astype(F32)
-    grad_qkv_ref[:, pl.ds(2 * C, C)] = gathered[0].astype(F32)
-    wait_received(gathered.at[3 - core], BOTH_SEM + 1)
-    for j in range(2):
-        part = pl.ds(j * C, C)
-        grad_qkv_ref[:, part] = gathered[2 + j].astype(F32)
+
+    @pl.when(core == 0)
+    def _():
+        deliver_half(1)
+
+    @pl.when(core == 1)
+    def _():
+        deliver_half(0)
 
     wait_sent(halo, HALO_SEM)
     wait_sent(grad_send, BACK_SEM)
     wait_sent(small_own, SMALL_CORE)
+    wait_sent(gathered.at[0, pl.ds(0, NP - 1)], GATHER_SEM)
+    wait_sent(own_half, BOTH_SEM)
     for stage in range(2):
         wait_sent(core_send.at[stage], CORE_SEM + stage)
         wait_sent(plane_recv.at[stage], PLANE_SEM + stage)
-        wait_sent(gathered.at[0, pl.ds(0, 240)], GATHER_SEM + stage)
-        wait_sent(gathered.at[0], BOTH_SEM + stage)
-
-    @pl.when(z != 0)
+
+    @pl.when(z >= OWNER_PLANES)
+    def _():
+        for stage in range(2):
+            wait_sent(line_recv.at[stage, pl.ds(0, OWNER_PLANES)], LINE_SEM + stage)
+
+    @pl.when(z < OWNER_PLANES)
     def _():
         for stage in range(2):
             wait_sent(line_send.at[stage], LINE_SEM + stage)
 
-    @pl.when(z == 0)
-    def _():
-        for stage in range(2):
-            wait_sent(line_recv.at[stage, pl.ds(1, NZ - 1)], CAST_SEM + stage)
+    for owner in range(OWNER_PLANES):
+
+        @pl.when(z == owner)
+        def _():
+            wait_sent(gathered.at[0, pl.ds(0, len(CASTS[owner]))], CAST_SEM)
 
     @pl.when(chip != 0)
     def _():
@@ -535,15 +596,21 @@
 
     @pl.when(chip == 0)
     def _():
-        wait_sent(small_plane.at[pl.ds(1, NP - 1)], SMALL_GATHER)
-
-        @pl.when(z != 0)
+        wait_sent(small_plane.at[pl.ds(0, NP - 1)], SMALL_GATHER)
+
+        @pl.when(z >= OWNER_PLANES)
+        def _():
+            wait_sent(small_line.at[pl.ds(0, OWNER_PLANES)], SMALL_LINE)
+
+        @pl.when(z < OWNER_PLANES)
         def _():
             wait_sent(small_total, SMALL_LINE)
 
-        @pl.when(z == 0)
-        def _():
-            wait_sent(small_line.at[pl.ds(1, NZ - 1)], SMALL_CAST)
+        for owner in range(OWNER_PLANES):
+
+            @pl.when(z == owner)
+            def _():
+                wait_sent(small_line.at[pl.ds(0, len(CASTS[owner]))], SMALL_CAST)
 
 
 def deliver(
@@ -627,12 +694,12 @@
             pltpu.VMEM((2, NP - 1, 16, C), BF16),
             pltpu.VMEM((2, 16, C), BF16),
             pltpu.VMEM((2, NZ, 16, C), BF16),
-            pltpu.VMEM((4, C, C), BF16),
+            pltpu.VMEM((2, NP, 2, 16, C), BF16),
             pltpu.VMEM((8, OWN), F32),
             pltpu.VMEM((8, OWN), F32),
             pltpu.VMEM((NP, 8, OWN), F32),
             pltpu.VMEM((NZ, 8, OWN), F32),
-            pltpu.SemaphoreType.DMA((38,)),
+            pltpu.SemaphoreType.DMA((32,)),
             pltpu.SemaphoreType.DMA((6,)),
         ],
         compiler_params=pltpu.CompilerParams(

time: 46.4 us -> 45.5 us (0.981)
  the two profiles are of different devices: /device:TPU:33 before, /device:TPU:1 now
where the time goes in v4:
time: 45.5 us; the launch traced here: 45.2 us
  Pallas kernels  44.5 us (98%)
  between operations  0.64 us (1%)
    pallas_call x1, Pallas kernels, on_device(): pl.pallas_call(kernel, out_shape=(pltpu.VMEM((OWN, C), BF16), pltpu.VMEM(...  43.5 us
    pallas_call x1, Pallas kernels, on_device(): pl.pallas_call(deliver, out_shape=(jax.ShapeDtypeStruct((OWN, C), BF16),...  1.06 us

profile of v4, /device:TPU:1, one launch (start us, length us, event | category | flops | bytes accessed | tf_op | source)
XLA Modules:
  0.0 45.2 jit_solution(6223333753011662337)
XLA Ops:
  0.6 43.5 %shard_map.109 = (bf16[128,256]{1,0:T(8,128)(2,1)S(1)}, bf16[128,256]{1,0:T(8,128)(2,1)S(1)}, f32[256,768]{1,0:T(8,128)S(1)}, f32[256,256]{1,0:T(8,128)S(1)}, f32[8,128]{1,0:T(8,128)S(1)}) custom-call(bf16[128,256]{1,0:T(8,128)(2,1)} %bitcast.8, bf16[256,768]{1,0:T(8,128)(2,1)} %refs_1_.1, bf16[256,256]{1,0:T(8,128)(2,1)} %refs_2_.1, f32[1,256]{1,0:T(1,128)} %bitcast.10, ...), custom_call_target="tpu_custom_call" | custom-call | tf_op jit(solution)/shard_map/pallas_call | solution.py:665
  44.1 1.1 %shard_map.110 = (bf16[128,256]{1,0:T(8,128)(2,1)}, bf16[128,256]{1,0:T(8,128)(2,1)}, f32[256,768]{1,0:T(8,128)}, f32[256,256]{1,0:T(8,128)}, f32[1,256]{1,0:T(1,128)}, /*index=5*/f32[1,4]{1,0:T(1,128)}) custom-call(bf16[128,256]{1,0:T(8,128)(2,1)S(1)} %get-tuple-element.17.output, bf16[128,256]{1,0:T(8,128)(2,1)S(1)} %get-tuple-element.18.grad_image, ...), custom_call_target="tpu_custom_call" | custom-call | tf_op jit(solution)/shard_map/pallas_call | solution.py:721

commit v5 on v4

--- a/solution.py
+++ b/solution.py
@@ -43,7 +43,7 @@
 )
 OWNER_PLANES = 2
 CASTS = ((10, 11, 12, 13, 14, 15), (2, 3, 4, 5, 6, 7, 8, 9))
-CASTS_FIRST = (2, 4)
+CASTS_FIRST = 4
 HALO_SEM, BACK_SEM, SMALL_CORE, SMALL_PLANE, SMALL_LINE, SMALL_CAST, SMALL_GATHER = range(7)
 CAST_SEM, GATHER_SEM, BOTH_SEM = range(7, 10)
 CORE_SEM, PLANE_SEM, LINE_SEM = range(10, 16, 2)
@@ -346,13 +346,12 @@
             line_recv[stage, z] = summed
             remote(line_send.at[stage], slot, LINE_SEM + stage, z_id(1 - z)).start()
 
-    def cast(ref, sem, ahead):
+    def cast(ref, sem, first, last):
         for owner in range(OWNER_PLANES):
 
             @pl.when(z == owner)
             def _():
-                first = CASTS_FIRST[owner]
-                for k in CASTS[owner][:first] if ahead else CASTS[owner][first:]:
+                for k in CASTS[owner][first:last]:
                     remote(ref, ref, sem, z_id(k)).start()
 
     spot = gathered.at[core, chip]
@@ -368,13 +367,13 @@
                     summed = summed + line_recv[stage, k].astype(F32)
                 gathered[core, chip, stage] = (summed * factor).astype(BF16)
 
-        cast(spot, CAST_SEM, True)
-
         @pl.when(z >= OWNER_PLANES)
         def _():
             wait_received(spot, CAST_SEM)
 
-        for other, device in peers:
+        for i, (other, device) in enumerate(peers):
+            if i % 4 == 0:
+                cast(spot, CAST_SEM, i // 4, i // 4 + 1)
             remote(spot, spot, GATHER_SEM, device).start()
 
     def deliver_half(side):
@@ -516,6 +515,7 @@
     grad_image_ref[...] = grad_image.astype(BF16)
 
     start_gather()
+    cast(spot, CAST_SEM, CASTS_FIRST, NZ)
 
     @pl.when(chip == 0)
     def _():
@@ -527,7 +527,7 @@
                 line = line + small_line[k]
             small_total[...] = line * factor
 
-        cast(small_total, SMALL_CAST, True)
+        cast(small_total, SMALL_CAST, 0, CASTS_FIRST)
 
         @pl.when(z >= OWNER_PLANES)
         def _():
@@ -536,9 +536,7 @@
         for other, device in peers:
             remote(small_total, small_total, SMALL_GATHER, device).start()
 
-        cast(small_total, SMALL_CAST, False)
-
-    cast(spot, CAST_SEM, False)
+        cast(small_total, SMALL_CAST, CASTS_FIRST, NZ)
 
     wait_received(gathered.at[0, pl.ds(0, NP - 1)], GATHER_SEM)
     remote(own_half, own_half, BOTH_SEM, sibling).start()

time: 45.5 us -> 45.5 us (level)
  no operation moved by 1% of the time
where the time goes in v5:
time: 45.5 us; the launch traced here: 45.2 us
  Pallas kernels  44.5 us (98%)
  between operations  0.64 us (1%)
    pallas_call x1, Pallas kernels, on_device(): pl.pallas_call(kernel, out_shape=(pltpu.VMEM((OWN, C), BF16), pltpu.VMEM(...  43.5 us
    pallas_call x1, Pallas kernels, on_device(): pl.pallas_call(deliver, out_shape=(jax.ShapeDtypeStruct((OWN, C), BF16),...  1.06 us

profile of v5, /device:TPU:1, one launch (start us, length us, event | category | flops | bytes accessed | tf_op | source)
XLA Modules:
  0.0 45.2 jit_solution(12679966897990262724)
XLA Ops:
  0.6 43.5 %shard_map.109 = (bf16[128,256]{1,0:T(8,128)(2,1)S(1)}, bf16[128,256]{1,0:T(8,128)(2,1)S(1)}, f32[256,768]{1,0:T(8,128)S(1)}, f32[256,256]{1,0:T(8,128)S(1)}, f32[8,128]{1,0:T(8,128)S(1)}) custom-call(bf16[128,256]{1,0:T(8,128)(2,1)} %bitcast.8, bf16[256,768]{1,0:T(8,128)(2,1)} %refs_1_.1, bf16[256,256]{1,0:T(8,128)(2,1)} %refs_2_.1, f32[1,256]{1,0:T(1,128)} %bitcast.10, ...), custom_call_target="tpu_custom_call" | custom-call | tf_op jit(solution)/shard_map/pallas_call | solution.py:663
  44.1 1.1 %shard_map.110 = (bf16[128,256]{1,0:T(8,128)(2,1)}, bf16[128,256]{1,0:T(8,128)(2,1)}, f32[256,768]{1,0:T(8,128)}, f32[256,256]{1,0:T(8,128)}, f32[1,256]{1,0:T(1,128)}, /*index=5*/f32[1,4]{1,0:T(1,128)}) custom-call(bf16[128,256]{1,0:T(8,128)(2,1)S(1)} %get-tuple-element.17.output, bf16[128,256]{1,0:T(8,128)(2,1)S(1)} %get-tuple-element.18.grad_image, ...), custom_call_target="tpu_custom_call" | custom-call | tf_op jit(solution)/shard_map/pallas_call | solution.py:719

commit v6 on v5

--- a/solution.py
+++ b/solution.py
@@ -180,10 +180,6 @@
         for k in range(1, NZ):
             greet(z_id(lax.rem(z + k, NZ)))
 
-    @pl.when(z >= OWNER_PLANES)
-    def _():
-        greet(z_id(jnp.where(z >= 10, 0, 1)))
-
     def remote(src, dst, sem, device):
         return pltpu.make_async_remote_copy(
             src_ref=src,
@@ -204,15 +200,8 @@
     loads[0].wait()
     side[...] = dot(sel, image_ref[...]).astype(BF16)
 
-    @pl.when(z >= OWNER_PLANES)
-    def _():
-        pl.semaphore_wait(barrier, 8 + (NP - 1) + OWNER_PLANES)
-
-    for owner in range(OWNER_PLANES):
-
-        @pl.when(z == owner)
-        def _():
-            pl.semaphore_wait(barrier, 8 + (NP - 1) + 1 + len(CASTS[owner]))
+    owners = OWNER_PLANES - jnp.where(z < OWNER_PLANES, 1, 0)
+    pl.semaphore_wait(barrier, 8 + (NP - 1) + owners)
 
     for place, step in reversed(tuple(zip(PLACES, OWNERS))):
         first, count = place[0], place[1]

time: 45.5 us -> 45.5 us (level)
  no operation moved by 1% of the time
where the time goes in v6:
time: 45.5 us; the launch traced here: 45.2 us
  Pallas kernels  44.5 us (98%)
  between operations  0.64 us (1%)
    pallas_call x1, Pallas kernels, on_device(): pl.pallas_call(kernel, out_shape=(pltpu.VMEM((OWN, C), BF16), pltpu.VMEM(...  43.5 us
    pallas_call x1, Pallas kernels, on_device(): pl.pallas_call(deliver, out_shape=(jax.ShapeDtypeStruct((OWN, C), BF16),...  1.06 us

profile of v6, /device:TPU:1, one launch (start us, length us, event | category | flops | bytes accessed | tf_op | source)
XLA Modules:
  0.0 45.2 jit_solution(13511831828931886016)
XLA Ops:
  0.6 43.5 %shard_map.109 = (bf16[128,256]{1,0:T(8,128)(2,1)S(1)}, bf16[128,256]{1,0:T(8,128)(2,1)S(1)}, f32[256,768]{1,0:T(8,128)S(1)}, f32[256,256]{1,0:T(8,128)S(1)}, f32[8,128]{1,0:T(8,128)S(1)}) custom-call(bf16[128,256]{1,0:T(8,128)(2,1)} %bitcast.8, bf16[256,768]{1,0:T(8,128)(2,1)} %refs_1_.1, bf16[256,256]{1,0:T(8,128)(2,1)} %refs_2_.1, f32[1,256]{1,0:T(1,128)} %bitcast.10, ...), custom_call_target="tpu_custom_call" | custom-call | tf_op jit(solution)/shard_map/pallas_call | solution.py:652
  44.1 1.1 %shard_map.110 = (bf16[128,256]{1,0:T(8,128)(2,1)}, bf16[128,256]{1,0:T(8,128)(2,1)}, f32[256,768]{1,0:T(8,128)}, f32[256,256]{1,0:T(8,128)}, f32[1,256]{1,0:T(1,128)}, /*index=5*/f32[1,4]{1,0:T(1,128)}) custom-call(bf16[128,256]{1,0:T(8,128)(2,1)S(1)} %get-tuple-element.17.output, bf16[128,256]{1,0:T(8,128)(2,1)S(1)} %get-tuple-element.18.grad_image, ...), custom_call_target="tpu_custom_call" | custom-call | tf_op jit(solution)/shard_map/pallas_call | solution.py:708
